TPU v7x, 256 devices: a whole 4x4x8 slice. The times are simulated.
256 devices in a mesh: ctx: 64 (over z, y, core), tp: 4 (over x).
Axes of the slice: x: 4, y: 4, z: 8, core: 2. Of those that a mesh axis runs over, the one named last changes fastest.
Arguments:
- xs: bfloat16 [8192, 8192], P(('ctx', 'tp')), may hold values from -6 to 6
- dts: bfloat16 [8192, 128], P(('ctx', 'tp')), may hold values from 0 to 0.35, as said below
- bs: bfloat16 [8192, 1024], P(('ctx', 'tp')), may hold values from -6 to 6
- cs: bfloat16 [8192, 1024], P(('ctx', 'tp')), may hold values from -6 to 6
- rates: float32 [128], P('tp'), may hold values from 0.5 to 2
- skips: float32 [128], P('tp'), may hold values from 0.5 to 1.5
- queries: bfloat16 [8192, 4096], P(('ctx', 'tp')), may hold values from -6 to 6
- keys: bfloat16 [8192, 1024], P(('ctx', 'tp')), may hold values from -6 to 6
- values: bfloat16 [8192, 1024], P(('ctx', 'tp')), may hold values from -6 to 6
- lengths: int32 [64], replicated, may hold values from 1 to 2048, 8192 in all
- grad_y: bfloat16 [8192, 8192], P(('ctx', 'tp')), may hold values from -6 to 6
- grad_attn: bfloat16 [8192, 4096], P(('ctx', 'tp')), may hold values from -6 to 6
Outputs:
- mixed_y: bfloat16 [8192, 8192], P(('ctx', 'tp'))
- grad_x: bfloat16 [8192, 8192], P(('ctx', 'tp'))
- grad_b: bfloat16 [8192, 1024], P(('ctx', 'tp'))
- grad_c: bfloat16 [8192, 1024], P(('ctx', 'tp'))
- attended: bfloat16 [8192, 4096], P(('ctx', 'tp'))
- grad_q: bfloat16 [8192, 4096], P(('ctx', 'tp'))
- grad_k: bfloat16 [8192, 1024], P(('ctx', 'tp'))
- grad_v: bfloat16 [8192, 1024], P(('ctx', 'tp'))
Inputs may be any that keep to these rules, and one draw needn't show every extreme that they name: `lengths`: 64 documents in order that together cover all 8192 tokens; one of them is exactly 2048 tokens long. `dts`: positive step sizes.
All inputs are finite; a program needn't handle non-finite values.
Results may differ from a plain program's by a relative error of at most 0.034.
Values may be sent and summed in bfloat16 or wider, within the bound.
No kernel may reach another device: no remote copies, remote signals or barrier semaphores. Data moves between devices by JAX's collectives and lax.ppermute only.
A program may use at most 384 MiB of HBM per device.

v0:
```python
import jax
import jax.numpy as jnp
from jax import lax
from jax.experimental import pallas as pl
from jax.experimental.pallas import tpu as pltpu
from jax.sharding import Mesh, PartitionSpec as P

BF = jnp.bfloat16
F32 = jnp.float32
GROUP = ("y", "core", "tp")
ROWS = 32
SUPER = 1024
BLOCK = 128
BLOCKS = SUPER // BLOCK
HEADS = 4
WIDTH = 64
CH = HEADS * WIDTH
STATE = 128
LANES = 128
SCALE = 128 ** (-0.5)
TQ = 256
TK = 512
NEG = -1e30
VMEM = 60 * 1024 * 1024
NN = (((1,), (0,)), ((), ()))
NT = (((1,), (1,)), ((), ()))
TN = (((0,), (0,)), ((), ()))


def dot(a, b, dims=NN):
    return lax.dot_general(a, b, dims, preferred_element_type=F32)


def params():
    return pltpu.CompilerParams(vmem_limit_bytes=VMEM)


def smem():
    return pl.BlockSpec(memory_space=pltpu.SMEM)


def vmem():
    return pl.BlockSpec(memory_space=pltpu.VMEM)


def pack_mixer(x_ref, gy_ref, b_ref, c_ref, dt_ref, out_ref):
    for t in range(4):
        out_ref[t, :, 0:256] = x_ref[:, t * 256 : t * 256 + 256]
        out_ref[t, :, 256:512] = gy_ref[:, t * 256 : t * 256 + 256]
        out_ref[t, :, 512:640] = b_ref[...]
        out_ref[t, :, 640:768] = c_ref[...]
        out_ref[t, :, 768:896] = dt_ref[...]


def pack_attention(q_ref, ga_ref, k2, v2, k1, v1, k0, v0, out_ref):
    for t in range(4):
        out_ref[t, :, 0:128] = q_ref[:, t * 128 : t * 128 + 128]
        out_ref[t, :, 128:256] = ga_ref[:, t * 128 : t * 128 + 128]
        for n, ref in enumerate((k2, v2, k1, v1, k0, v0)):
            out_ref[t, :, 256 + n * 128 : 384 + n * 128] = ref[...]


def wide(width, place=0):
    return pl.BlockSpec((ROWS, width), lambda g: (0, g + place))


def do_pack_mixer(xs, gy, bs, cs, dts):
    return pl.pallas_call(
        pack_mixer,
        grid=(8,),
        in_specs=[wide(1024), wide(1024), wide(128), wide(128), pl.BlockSpec((ROWS, 128), lambda g: (0, 0))],
        out_specs=pl.BlockSpec((4, ROWS, 896), lambda g: (g, 0, 0)),
        out_shape=jax.ShapeDtypeStruct((32, ROWS, 896), BF),
        compiler_params=params(),
    )(xs, gy, bs, cs, dts)


def do_pack_attention(q, ga, kv2, kv1, kv0):
    return pl.pallas_call(
        pack_attention,
        grid=(8,),
        in_specs=[wide(512), wide(512)] + [wide(128), wide(128, 8)] * 3,
        out_specs=pl.BlockSpec((4, ROWS, 1024), lambda g: (g, 0, 0)),
        out_shape=jax.ShapeDtypeStruct((32, ROWS, 1024), BF),
        compiler_params=params(),
    )(q, ga, kv2, kv2, kv1, kv1, kv0, kv0)


def unpack_mixer(in_ref, y_ref, gx_ref, gb_ref, gc_ref):
    gb = jnp.zeros((ROWS, 128), F32)
    gc = jnp.zeros((ROWS, 128), F32)
    for t in range(4):
        y_ref[:, t * 256 : t * 256 + 256] = in_ref[t, :, 0:256]
        gx_ref[:, t * 256 : t * 256 + 256] = in_ref[t, :, 256:512]
        gb = gb + in_ref[t, :, 512:640].astype(F32)
        gc = gc + in_ref[t, :, 640:768].astype(F32)
    gb_ref[...] = gb.astype(BF)
    gc_ref[...] = gc.astype(BF)


def do_unpack_mixer(got):
    return pl.pallas_call(
        unpack_mixer,
        grid=(8,),
        in_specs=[pl.BlockSpec((4, ROWS, 768), lambda g: (g, 0, 0))],
        out_specs=[wide(1024), wide(1024), wide(128), wide(128)],
        out_shape=[
            jax.ShapeDtypeStruct((ROWS, 8192), BF),
            jax.ShapeDtypeStruct((ROWS, 8192), BF),
            jax.ShapeDtypeStruct((ROWS, 1024), BF),
            jax.ShapeDtypeStruct((ROWS, 1024), BF),
        ],
        compiler_params=params(),
    )(got)


def unpack_attention(in_ref, att_ref, gq_ref, kv2_ref, kv1_ref, kv0_ref):
    for t in range(4):
        att_ref[:, t * 128 : t * 128 + 128] = in_ref[t, :, 0:128]
        gq_ref[:, t * 128 : t * 128 + 128] = in_ref[t, :, 128:256]
    for n, ref in enumerate((kv2_ref, kv1_ref, kv0_ref)):
        total = in_ref[0, :, 256 + n * 256 : 512 + n * 256].astype(F32)
        for t in range(1, 4):
            total = total + in_ref[t, :, 256 + n * 256 : 512 + n * 256].astype(F32)
        ref[...] = total.astype(ref.dtype)


def do_unpack_attention(got):
    return pl.pallas_call(
        unpack_attention,
        grid=(8,),
        in_specs=[pl.BlockSpec((4, ROWS, 1024), lambda g: (g, 0, 0))],
        out_specs=[wide(512), wide(512), wide(256), wide(256), wide(256)],
        out_shape=[
            jax.ShapeDtypeStruct((ROWS, 4096), BF),
            jax.ShapeDtypeStruct((ROWS, 4096), BF),
            jax.ShapeDtypeStruct((ROWS, 2048), BF),
            jax.ShapeDtypeStruct((ROWS, 2048), BF),
            jax.ShapeDtypeStruct((ROWS, 2048), F32),
        ],
        compiler_params=params(),
    )(got)


def add_kv(own_ref, one_ref, two_ref, gk_ref, gv_ref):
    for g in range(8):
        at = slice(g * 256, g * 256 + 256)
        total = (own_ref[:, at] + one_ref[:, at].astype(F32) + two_ref[:, at].astype(F32)).astype(BF)
        gk_ref[:, g * 128 : g * 128 + 128] = total[:, 0:128]
        gv_ref[:, g * 128 : g * 128 + 128] = total[:, 128:256]


def do_add_kv(own, one, two):
    return pl.pallas_call(
        add_kv,
        in_specs=[vmem()] * 3,
        out_specs=[vmem()] * 2,
        out_shape=[jax.ShapeDtypeStruct((ROWS, 1024), BF)] * 2,
        compiler_params=params(),
    )(own, one, two)


def lane_row(values, width):
    lane = lax.broadcasted_iota(jnp.int32, (1, width * HEADS), 1)
    row = jnp.full((1, width * HEADS), values[0], F32)
    for h in range(1, HEADS):
        row = jnp.where(lane >= h * width, values[h], row)
    return row


def lower(n):
    return (
        lax.broadcasted_iota(jnp.int32, (n, n), 1) <= lax.broadcasted_iota(jnp.int32, (n, n), 0)
    ).astype(F32).astype(BF)


def upper(n):
    return (
        lax.broadcasted_iota(jnp.int32, (n, n), 0) <= lax.broadcasted_iota(jnp.int32, (n, n), 1)
    ).astype(F32).astype(BF)


def pick(first, width):
    head = lax.broadcasted_iota(jnp.int32, (128, width * HEADS), 0) - first
    lane = lax.broadcasted_iota(jnp.int32, (128, width * HEADS), 1) // width
    return (head == lane).astype(F32).astype(BF)


def channel_decay(dts, chooser, tri, rate_row, tail, entry):
    steps = dot(dts, chooser)
    cumul = dot(tri, steps.astype(BF)) * (-rate_row)
    end = cumul[BLOCK - 1 : BLOCK, :]
    row = lax.broadcasted_iota(jnp.int32, (BLOCK, CH), 0)
    weight = jnp.where(row >= tail, jnp.exp(end - cumul), 0.0)
    enter = jnp.where(row < entry, jnp.exp(cumul), 0.0)
    return steps, steps * weight, enter, end


def state_kernel(info, rates, in_ref, inc_ref, out_ref, factor_ref, sf_ref, sb_ref):
    first = info[3, 0] * HEADS
    tri = lower(BLOCK)
    chooser = pick(first, WIDTH)
    rate_row = lane_row([rates[h] for h in range(HEADS)], WIDTH)
    state = jnp.zeros((STATE, CH), F32)
    prefix = jnp.ones((1, CH), F32)
    carries = []
    pulled = []
    for j in range(BLOCKS):
        rows = slice(j * BLOCK, j * BLOCK + BLOCK)
        tail, entry, alive = info[0, j], info[1, j], info[2, j]
        _, weighted, enter, end = channel_decay(
            in_ref[rows, 768:896], chooser, tri, rate_row, tail, entry
        )
        scaled = (in_ref[rows, 0:256].astype(F32) * weighted).astype(BF)
        dcar = (in_ref[rows, 256:512].astype(F32) * enter).astype(BF)
        carry = jnp.where(alive > 0, jnp.exp(end), 0.0)
        inc_ref[j] = state
        factor_ref[j : j + 1, :] = prefix
        state = carry * state + dot(in_ref[rows, 512:640], scaled, TN)
        prefix = prefix * carry
        carries.append(carry)
        pulled.append(dot(in_ref[rows, 640:768], dcar, TN))
    high = prefix.astype(BF)
    low = (prefix - high.astype(F32)).astype(BF)
    place = lax.broadcasted_iota(jnp.int32, (16, CH), 0)
    extra = jnp.where(place == 0, high.astype(F32), jnp.where(place == 1, low.astype(F32), 0.0)).astype(BF)
    sf_ref[0:128, :] = state.astype(BF)
    sf_ref[128:144, :] = extra
    back = jnp.zeros((STATE, CH), F32)
    suffix = jnp.ones((1, CH), F32)
    for j in range(BLOCKS - 1, -1, -1):
        out_ref[j] = back
        factor_ref[8 + j : 9 + j, :] = suffix
        back = pulled[j] + carries[j] * back
        suffix = suffix * carries[j]
    sb_ref[0:128, :] = back.astype(BF)
    sb_ref[128:144, :] = extra


def do_state(info, rates, got):
    return pl.pallas_call(
        state_kernel,
        in_specs=[smem(), smem(), vmem()],
        out_specs=[vmem()] * 5,
        out_shape=[
            jax.ShapeDtypeStruct((BLOCKS, STATE, CH), F32),
            jax.ShapeDtypeStruct((BLOCKS, STATE, CH), F32),
            jax.ShapeDtypeStruct((16, CH), F32),
            jax.ShapeDtypeStruct((144, CH), BF),
            jax.ShapeDtypeStruct((144, CH), BF),
        ],
        compiler_params=params(),
    )(info, rates, got)


def joined(one_ref, two_ref):
    decay = one_ref[128:129, :].astype(F32) + one_ref[129:130, :].astype(F32)
    return one_ref[0:128, :].astype(F32) + decay * two_ref[0:128, :].astype(F32)


def mixer_kernel(
    info, rates, skips, in_ref, ends_ref, inc_ref, back_ref, factor_ref, f1, f2, b1, b2, out_ref
):
    first = info[3, 0] * HEADS
    tri = lower(BLOCK)
    triu = upper(BLOCK)
    chooser = pick(first, WIDTH)
    column_chooser = pick(first, LANES)
    head_row = lax.broadcasted_iota(jnp.int32, (8, 128), 0)
    head_at = lax.broadcasted_iota(jnp.int32, (8, 128), 1) - first
    row_chooser = ((head_row == head_at) & (head_row < HEADS)).astype(F32).astype(BF)
    rate_row = lane_row([rates[h] for h in range(HEADS)], WIDTH)
    skip_row = lane_row([skips[h] for h in range(HEADS)], WIDTH)
    entering = joined(f1, f2)
    leaving = joined(b1, b2)
    t_at = lax.broadcasted_iota(jnp.int32, (BLOCK, BLOCK), 0)
    s_at = lax.broadcasted_iota(jnp.int32, (BLOCK, BLOCK), 1)
    lane = lax.broadcasted_iota(jnp.int32, (BLOCK, CH), 1)
    owns = [(lane >= h * WIDTH) & (lane < (h + 1) * WIDTH) for h in range(HEADS)]

    def one(j, _):
        rows = pl.ds(pl.multiple_of(j * BLOCK, BLOCK), BLOCK)
        tail, entry = info[0, j], info[1, j]
        dts = in_ref[rows, 768:896]
        steps, weighted, enter, _ = channel_decay(dts, chooser, tri, rate_row, tail, entry)
        x = in_ref[rows, 0:256].astype(F32)
        gy_low = in_ref[rows, 256:512]
        gy = gy_low.astype(F32)
        b = in_ref[rows, 512:640]
        c = in_ref[rows, 640:768]
        state = (inc_ref[j] + factor_ref[pl.ds(j, 1), :] * entering).astype(BF)
        pull = (back_ref[j] + factor_ref[pl.ds(8 + j, 1), :] * leaving).astype(BF)
        columns = dot(tri, dot(dts, column_chooser).astype(BF))
        lines = dot(dot(row_chooser, dts, NT).astype(BF), triu)
        ends = ends_ref[pl.ds(j, 1), :]
        mask = (s_at <= t_at) & (t_at < ends)
        scores = dot(c, b, NT)
        driven = x * steps
        decays = []
        mixes = []
        drives = []
        for h in range(HEADS):
            gap = (columns[:, h * 128 : h * 128 + 128] - lines[h : h + 1, :]) * (-rates[h])
            decay = jnp.exp(jnp.where(mask, gap, NEG))
            decays.append(decay)
            mixes.append((decay * scores).astype(BF))
            drives.append(jnp.where(owns[h], driven, 0.0).astype(BF))
        mix = jnp.concatenate(mixes, axis=1)
        drive = jnp.concatenate(drives, axis=0)
        y = dot(mix, drive) + dot(c, state) * enter + skip_row * x
        out_ref[rows, 0:256] = y.astype(BF)
        grad_mix = dot(gy_low, drive, NT)
        grad_scores = decays[0] * grad_mix[:, 0:128]
        for h in range(1, HEADS):
            grad_scores = grad_scores + decays[h] * grad_mix[:, h * 128 : h * 128 + 128]
        grad_low = grad_scores.astype(BF)
        back = dot(mix, gy_low, TN)
        grad_drive = jnp.where(owns[0], back[0:128], 0.0)
        for h in range(1, HEADS):
            grad_drive = jnp.where(owns[h], back[h * 128 : h * 128 + 128], grad_drive)
        grad_scaled = dot(b, pull)
        gx = grad_drive * steps + grad_scaled * weighted + skip_row * gy
        out_ref[rows, 256:512] = gx.astype(BF)
        scaled = (x * weighted).astype(BF)
        dcar = (gy * enter).astype(BF)
        gb = dot(grad_low, c, TN) + dot(scaled, pull, NT)
        gc = dot(grad_low, b) + dot(dcar, state, NT)
        out_ref[rows, 512:640] = gb.astype(BF)
        out_ref[rows, 640:768] = gc.astype(BF)
        return 0

    lax.fori_loop(0, BLOCKS, one, 0)


def do_mixer(info, rates, skips, got, ends, inc, back, factor, f1, f2, b1, b2):
    return pl.pallas_call(
        mixer_kernel,
        in_specs=[smem()] * 3 + [vmem()] * 9,
        out_specs=vmem(),
        out_shape=jax.ShapeDtypeStruct((SUPER, 768), BF),
        compiler_params=params(),
    )(info, rates, skips, got, ends, inc, back, factor, f1, f2, b1, b2)


def attention_kernel(starts, in_ref, start_ref, out_ref, kt_ref, vt_ref, s_ref, acc_ref):
    tiles = 3 * SUPER // TK
    lowest = starts[0] // TK

    def key_at(t):
        rows = pl.ds(pl.multiple_of((t % 2) * TK, TK), TK)
        return rows, pl.multiple_of(256 + (t // 2) * 256, 256)

    def turn(t, _):
        rows, col = key_at(t)
        kt_ref[t] = in_ref[rows, pl.ds(col, 128)].T
        vt_ref[t] = in_ref[rows, pl.ds(col + 128, 128)].T
        return 0

    lax.fori_loop(lowest, tiles, turn, 0)
    acc_ref[...] = jnp.zeros_like(acc_ref)

    def one(i, _):
        rows = pl.ds(pl.multiple_of(i * TQ, TQ), TQ)
        q = in_ref[rows, 0:128]
        ga = in_ref[rows, 128:256]
        begin = start_ref[pl.ds(i, 1), :]
        here = 2 * SUPER + i * TQ + lax.broadcasted_iota(jnp.int32, (1, TQ), 1)
        low = starts[i * TQ] // TK
        high = (2 * SUPER + i * TQ + TQ - 1) // TK + 1

        def score(t, peak):
            krows, col = key_at(t)
            s = dot(in_ref[krows, pl.ds(col, 128)], q, NT) * SCALE
            at = t * TK + lax.broadcasted_iota(jnp.int32, (TK, TQ), 0)
            s = jnp.where((at >= begin) & (at <= here), s, NEG)
            s_ref[t] = s
            return jnp.maximum(peak, jnp.max(s.reshape(TK // 8, 8, TQ), axis=0))

        peak = lax.fori_loop(low, high, score, jnp.full((8, TQ), NEG, F32))
        peak = jnp.max(peak, axis=0, keepdims=True)

        def weigh(t, carry):
            total, att = carry
            p = jnp.exp(s_ref[t] - peak)
            s_ref[t] = p
            total = total + jnp.sum(p.reshape(TK // 8, 8, TQ), axis=0)
            return total, att + dot(vt_ref[t], p.astype(BF))

        total, att = lax.fori_loop(
            low, high, weigh, (jnp.zeros((8, TQ), F32), jnp.zeros((128, TQ), F32))
        )
        inverse = 1.0 / jnp.sum(total, axis=0, keepdims=True)
        att = (att * inverse).T.astype(BF)
        out_ref[rows, 0:128] = att
        delta = jnp.sum((ga.astype(F32) * att.astype(F32)).T, axis=0, keepdims=True)

        def grads(t, gq):
            krows, col = key_at(t)
            probs = s_ref[t] * inverse
            dp = dot(in_ref[krows, pl.ds(col + 128, 128)], ga, NT)
            ds = (probs * (dp - delta)).astype(BF)
            acc_ref[t, :, 0:128] += dot(ds, q)
            acc_ref[t, :, 128:256] += dot(probs.astype(BF), ga)
            return gq + dot(kt_ref[t], ds)

        gq = lax.fori_loop(low, high, grads, jnp.zeros((128, TQ), F32))
        out_ref[rows, 128:256] = (gq * SCALE).T.astype(BF)
        return 0

    lax.fori_loop(0, SUPER // TQ, one, 0)
    for t in range(tiles):
        rows = slice((t % 2) * TK, (t % 2) * TK + TK)
        col = 256 + (t // 2) * 256
        out_ref[rows, col : col + 128] = (acc_ref[t, :, 0:128] * SCALE).astype(BF)
        out_ref[rows, col + 128 : col + 256] = acc_ref[t, :, 128:256].astype(BF)


def do_attention(starts, got):
    tiles = 3 * SUPER // TK
    return pl.pallas_call(
        attention_kernel,
        in_specs=[smem(), vmem(), vmem()],
        out_specs=vmem(),
        out_shape=jax.ShapeDtypeStruct((SUPER, 1024), BF),
        scratch_shapes=[
            pltpu.VMEM((tiles, 128, TK), BF),
            pltpu.VMEM((tiles, 128, TK), BF),
            pltpu.VMEM((tiles, TK, TQ), F32),
            pltpu.VMEM((tiles, TK, 256), F32),
        ],
        compiler_params=params(),
    )(starts, got, starts.reshape(SUPER // TQ, TQ))


def shifted(block, distance):
    count = lax.axis_size("z")
    route = [(i, i + distance) for i in range(count) if 0 <= i + distance < count]
    return lax.ppermute(block, "z", route)


def exchange(block):
    return lax.all_to_all(block, GROUP, split_axis=0, concat_axis=0, tiled=True)


def per_device(xs, dts, bs, cs, rates, skips, queries, keys, values, lengths, grad_y, grad_attn):
    z, y, core, tp = (lax.axis_index(a) for a in ("z", "y", "core", "tp"))
    device = (y * 2 + core) * 4 + tp

    kv0 = jnp.concatenate([keys, values], axis=1)
    kv1 = shifted(kv0, 1)
    kv2 = shifted(kv0, 2)
    side = lax.axis_size("tp")
    both = lax.ppermute(
        jnp.stack([rates, skips]),
        ("y", "tp"),
        [(a * side + b, b * side + a) for a in range(side) for b in range(side)],
    )
    mine = lax.dynamic_slice_in_dim(both, core * 16 + tp * HEADS, HEADS, 1)
    my_rates, my_skips = mine[0], mine[1]

    ends = jnp.cumsum(lengths)
    begins = ends - lengths
    base = z * SUPER
    positions = base + jnp.arange(SUPER, dtype=jnp.int32)
    starts = jnp.max(jnp.where(begins[None, :] <= positions[:, None], begins[None, :], 0), axis=1)
    stops = jnp.min(
        jnp.where(ends[None, :] > positions[:, None], ends[None, :], SUPER * 8), axis=1
    )
    block_at = base + jnp.arange(BLOCKS, dtype=jnp.int32) * BLOCK
    last_start = starts[BLOCK - 1 :: BLOCK]
    prior_stop = jnp.min(
        jnp.where(ends[None, :] >= block_at[:, None], ends[None, :], SUPER * 8), axis=1
    )
    entry = jnp.where(block_at > 0, prior_stop - block_at, 0)
    info = jnp.stack(
        [
            last_start - block_at,
            entry,
            (last_start < block_at).astype(jnp.int32),
            jnp.full((BLOCKS,), device, jnp.int32),
        ]
    )
    local_stops = (stops.reshape(BLOCKS, BLOCK) - block_at[:, None]).astype(jnp.int32)

    got = exchange(do_pack_mixer(xs, grad_y, bs, cs, dts)).reshape(SUPER, 896)
    inc, back, factor, send_f, send_b = do_state(info, my_rates, got)
    f1, f2 = shifted(send_f, 1), shifted(send_f, 2)
    b1, b2 = shifted(send_b, -1), shifted(send_b, -2)

    got_a = exchange(do_pack_attention(queries, grad_attn, kv2, kv1, kv0)).reshape(SUPER, 1024)
    attended = do_attention((starts - (base - 2 * SUPER)).astype(jnp.int32), got_a)
    out_a = exchange(attended.reshape(32, ROWS, 1024))
    att, gq, p2, p1, p0 = do_unpack_attention(out_a)
    r1, r2 = shifted(p1, -1), shifted(p2, -2)

    mixed = do_mixer(
        info, my_rates, my_skips, got, local_stops, inc, back, factor, f1, f2, b1, b2
    )
    out_m = exchange(mixed.reshape(32, ROWS, 768))
    y_out, gx, gb, gc = do_unpack_mixer(out_m)
    gk, gv = do_add_kv(p0, r1, r2)
    return y_out, gx, gb, gc, att, gq, gk, gv


def solution(mesh):
    fine = Mesh(mesh.devices.reshape(-1, 4, 2, 4), ("z", "y", "core", "tp"))
    rows = P(("z", "y", "core", "tp"), None)
    return jax.shard_map(
        per_device,
        mesh=fine,
        in_specs=(rows, rows, rows, rows, P("tp"), P("tp"), rows, rows, rows, P(), rows, rows),
        out_specs=(rows,) * 8,
        check_vma=False,
    )
```

profile of v0, /device:TPU:64, one launch (start us, length us, event | category | flops | bytes accessed | tf_op | source)
XLA Modules:
  0.0 197.9 jit_solution(9679173221238728102)
XLA Ops:
  0.6 0.8 constant_dynamic-update-slice_fusion.1
  1.5 0.8 constant_dynamic-update-slice_fusion.k0.v0
  2.3 6.4 %collective-permute-start.5 = (bf16[32,2048]{1,0:T(8,128)(2,1)S(1)}, bf16[32,2048]{1,0:T(8,128)(2,1)S(1)}, u32[]{:S(2)}, u32[]{:S(2)}) collective-permute-start(bf16[32,2048]{1,0:T(8,128)(2,1)S(1)} %constant_dynamic-update-slice_fusion.k0.v0), channel_id=1, source_target_pairs={{0,64},{32,96},{64,128},{96,160},{128,192},{160,224},{1,65},{33,97... | collective-permute-start | bytes 393224 | tf_op jit(solution)/shard_map/ppermute | solution.py:438
  8.7 2.9 %collective-permute-start.6 = (bf16[32,2048]{1,0:T(8,128)(2,1)S(1)}, bf16[32,2048]{1,0:T(8,128)(2,1)S(1)}, u32[]{:S(2)}, u32[]{:S(2)}) collective-permute-start(bf16[32,2048]{1,0:T(8,128)(2,1)S(1)} %constant_dynamic-update-slice_fusion.k0.v0), channel_id=1, source_target_pairs={{0,32},{32,64},{64,96},{96,128},{128,160},{160,192},{192,224},{1,3... | collective-permute-start | bytes 393224 | tf_op jit(solution)/shard_map/ppermute | solution.py:438
  11.6 3.5 %collective-permute-done.5.k2.v2 = bf16[32,2048]{1,0:T(8,128)(2,1)S(1)} collective-permute-done((bf16[32,2048]{1,0:T(8,128)(2,1)S(1)}, bf16[32,2048]{1,0:T(8,128)(2,1)S(1)}, u32[]{:S(2)}, u32[]{:S(2)}) %collective-permute-start.5) | collective-permute-done | bytes 131104 | tf_op jit(solution)/shard_map/ppermute | solution.py:438
  15.1 1.9 collective-permute-done.6.k1.v1
  17.0 0.0 copy-done.3
  17.0 0.0 copy-done.4
  17.0 0.7 copy-done.5
  17.7 5.2 %shard_map.183 = bf16[32,32,1024]{2,1,0:T(8,128)(2,1)} custom-call(bf16[32,4096]{1,0:T(8,128)(2,1)} %q_ref.1, bf16[32,4096]{1,0:T(8,128)(2,1)} %ga_ref.1, bf16[32,2048]{1,0:T(8,128)(2,1)} %copy-done.4, bf16[32,2048]{1,0:T(8,128)(2,1)} %copy-done.4, bf16[32,2048]{1,0:T(8,128)(2,1)} %copy-done.5, bf16[32,2048]{1,0:T(8,128)(2,1)} %copy-done.5, ...), custom_call_target="tpu_custom_call" | custom-call | tf_op jit(solution)/shard_map/pallas_call | solution.py:79
  22.9 7.3 %all-to-all-start.2 = ((bf16[32,32,1024]{2,1,0:T(8,128)(2,1)}), bf16[32,32,1024]{2,1,0:T(8,128)(2,1)S(1)}, u32[]{:S(2)}, u32[]{:S(2)}) async-start(bf16[32,32,1024]{2,1,0:T(8,128)(2,1)} %shard_map.183), calls=%async_computation.2 | async-start | bytes 4194304 | tf_op jit(solution)/shard_map/all_to_all | solution.py:442
  30.2 5.3 %shard_map.179 = bf16[32,32,896]{2,1,0:T(8,128)(2,1)} custom-call(bf16[32,8192]{1,0:T(8,128)(2,1)} %x_ref.1, bf16[32,8192]{1,0:T(8,128)(2,1)} %gy_ref.1, bf16[32,1024]{1,0:T(8,128)(2,1)} %b_ref.1, bf16[32,1024]{1,0:T(8,128)(2,1)} %c_ref.1, bf16[32,128]{1,0:T(8,128)(2,1)} %dt_ref.1), custom_call_target="tpu_custom_call" | custom-call | tf_op jit(solution)/shard_map/pallas_call | solution.py:68
  35.5 22.1 %all-to-all-done.2 = bf16[32,32,1024]{2,1,0:T(8,128)(2,1)S(1)} async-done(((bf16[32,32,1024]{2,1,0:T(8,128)(2,1)}), bf16[32,32,1024]{2,1,0:T(8,128)(2,1)S(1)}, u32[]{:S(2)}, u32[]{:S(2)}) %all-to-all-start.2) | async-done | bytes 2097184 | tf_op jit(solution)/shard_map/all_to_all | solution.py:442
  57.7 1.3 copy-done.1
  59.0 4.9 %all-to-all-start = ((bf16[32,32,896]{2,1,0:T(8,128)(2,1)}), bf16[32,32,896]{2,1,0:T(8,128)(2,1)S(1)}, u32[]{:S(2)}, u32[]{:S(2)}) async-start(bf16[32,32,896]{2,1,0:T(8,128)(2,1)} %shard_map.179), calls=%async_computation | async-start | bytes 3670016 | tf_op jit(solution)/shard_map/all_to_all | solution.py:442
  63.9 0.0 copy-done.13
  63.9 0.1 copy.22
  64.0 0.1 reduce-window.8
  64.1 0.1 reduce
  64.2 0.2 select_reduce_fusion
  64.4 0.0 copy-start.12
  64.4 0.6 sub.43.start_ref
  65.0 0.0 copy-done.12
  65.0 19.5 %shard_map.184 = bf16[1024,1024]{1,0:T(8,128)(2,1)} custom-call(s32[1024]{0:T(1024)} %copy-done.12, bf16[1024,1024]{1,0:T(8,128)(2,1)} %bitcast.25, s32[4,256]{1,0:T(4,128)} %sub.43.start_ref), custom_call_target="tpu_custom_call" | custom-call | tf_op jit(solution)/shard_map/pallas_call | solution.py:420
  84.6 4.3 %all-to-all-done = bf16[32,32,896]{2,1,0:T(8,128)(2,1)S(1)} async-done(((bf16[32,32,896]{2,1,0:T(8,128)(2,1)}), bf16[32,32,896]{2,1,0:T(8,128)(2,1)S(1)}, u32[]{:S(2)}, u32[]{:S(2)}) %all-to-all-start) | async-done | bytes 1835040 | tf_op jit(solution)/shard_map/all_to_all | solution.py:442
  88.9 1.2 copy-done
  90.2 4.8 %all-to-all-start.3 = ((bf16[32,32,1024]{2,1,0:T(8,128)(2,1)}), bf16[32,32,1024]{2,1,0:T(8,128)(2,1)}, u32[]{:S(2)}, u32[]{:S(2)}) async-start(bf16[32,32,1024]{2,1,0:T(8,128)(2,1)} %bitcast.24), calls=%async_computation.3 | async-start | bytes 4194304 | tf_op jit(solution)/shard_map/all_to_all | solution.py:442
  95.0 0.7 collective-permute-start
  95.6 0.1 slice.9
  95.7 0.1 pad.5.clone
  95.8 0.2 select_reduce_fusion.2
  96.0 0.6 add_add_fusion.info
  96.7 0.0 collective-permute-done
  96.7 0.1 constant_dynamic-slice_fusion
  96.8 0.5 slice_bitcast_fusion
  97.3 5.1 %shard_map.180 = (f32[8,128,256]{2,1,0:T(8,128)}, f32[8,128,256]{2,1,0:T(8,128)}, f32[16,256]{1,0:T(8,128)}, bf16[144,256]{1,0:T(8,128)(2,1)}, bf16[144,256]{1,0:T(8,128)(2,1)}) custom-call(s32[4,8]{1,0:T(4,128)} %add_add_fusion.info, f32[4]{0:T(128)} %get-tuple-element.43.rates, bf16[1024,896]{1,0:T(8,128)(2,1)} %bitcast.22), custom_call_target="tpu_custom_call" | custom-call | tf_op jit(solution)/shard_map/pallas_call | solution.py:241
  102.3 4.4 %collective-permute-start.1 = (bf16[144,256]{1,0:T(8,128)(2,1)}, bf16[144,256]{1,0:T(8,128)(2,1)S(1)}, u32[]{:S(2)}, u32[]{:S(2)}) collective-permute-start(bf16[144,256]{1,0:T(8,128)(2,1)} %get-tuple-element.27), channel_id=1, source_target_pairs={{0,32},{32,64},{64,96},{96,128},{128,160},{160,192},{192,224},{1,3... | collective-permute-start | bytes 221192 | tf_op jit(solution)/shard_map/ppermute | solution.py:438
  106.7 3.6 %collective-permute-start.2 = (bf16[144,256]{1,0:T(8,128)(2,1)}, bf16[144,256]{1,0:T(8,128)(2,1)S(1)}, u32[]{:S(2)}, u32[]{:S(2)}) collective-permute-start(bf16[144,256]{1,0:T(8,128)(2,1)} %get-tuple-element.27), channel_id=1, source_target_pairs={{0,64},{32,96},{64,128},{96,160},{128,192},{160,224},{1,65},{33,97... | collective-permute-start | bytes 221192 | tf_op jit(solution)/shard_map/ppermute | solution.py:438
  110.4 3.9 %collective-permute-start.3 = (bf16[144,256]{1,0:T(8,128)(2,1)}, bf16[144,256]{1,0:T(8,128)(2,1)S(1)}, u32[]{:S(2)}, u32[]{:S(2)}) collective-permute-start(bf16[144,256]{1,0:T(8,128)(2,1)} %get-tuple-element.28), channel_id=1, source_target_pairs={{32,0},{64,32},{96,64},{128,96},{160,128},{192,160},{224,192},{33,... | collective-permute-start | bytes 221192 | tf_op jit(solution)/shard_map/ppermute | solution.py:438
  114.3 1.9 collective-permute-start.4
  116.2 0.7 bitcast_subtract_fusion.ends_ref
  116.9 0.0 collective-permute-done.1.f1
  116.9 0.0 collective-permute-done.2.f2
  116.9 0.0 copy-start.9
  116.9 0.0 collective-permute-done.3.b1
  116.9 0.0 copy-start.10
  117.0 6.7 %collective-permute-done.4.b2 = bf16[144,256]{1,0:T(8,128)(2,1)S(1)} collective-permute-done((bf16[144,256]{1,0:T(8,128)(2,1)}, bf16[144,256]{1,0:T(8,128)(2,1)S(1)}, u32[]{:S(2)}, u32[]{:S(2)}) %collective-permute-start.4) | collective-permute-done | bytes 73760 | tf_op jit(solution)/shard_map/ppermute | solution.py:438
  123.7 0.0 copy-done.9
  123.7 0.6 copy-done.11
  124.3 11.7 %shard_map.181 = bf16[1024,768]{1,0:T(8,128)(2,1)} custom-call(s32[4,8]{1,0:T(4,128)} %add_add_fusion.info, f32[4]{0:T(128)} %get-tuple-element.43.rates, f32[4]{0:T(128)} %get-tuple-element.42.skips, bf16[1024,896]{1,0:T(8,128)(2,1)} %bitcast.23, s32[8,128]{1,0:T(8,128)} %bitcast_subtract_fusion.ends_ref, f32[8,128,256]{2,1,0:T(8,128)} %get-tuple-element.24.inc_ref, ...), custom_call_target="tpu_custom_call" | custom-call | tf_op jit(solution)/shard_map/pallas_call | solution.py:336
  135.9 0.0 all-to-all-done.3.in_ref
  136.0 30.5 %all-to-all-start.1 = ((bf16[32,32,768]{2,1,0:T(8,128)(2,1)}), bf16[32,32,768]{2,1,0:T(8,128)(2,1)S(1)}, u32[]{:S(2)}, u32[]{:S(2)}) async-start(bf16[32,32,768]{2,1,0:T(8,128)(2,1)} %bitcast.26), calls=%async_computation.1 | async-start | bytes 3145728 | tf_op jit(solution)/shard_map/all_to_all | solution.py:442
  166.5 5.4 %shard_map.185 = (bf16[32,4096]{1,0:T(8,128)(2,1)}, bf16[32,4096]{1,0:T(8,128)(2,1)}, bf16[32,2048]{1,0:T(8,128)(2,1)}, bf16[32,2048]{1,0:T(8,128)(2,1)}, f32[32,2048]{1,0:T(8,128)}) custom-call(bf16[32,32,1024]{2,1,0:T(8,128)(2,1)} %all-to-all-done.3.in_ref), custom_call_target="tpu_custom_call" | custom-call | tf_op jit(solution)/shard_map/pallas_call | solution.py:129
  171.9 1.9 collective-permute-start.7
  173.8 1.9 collective-permute-start.8
  175.7 13.2 %all-to-all-done.1.in_ref = bf16[32,32,768]{2,1,0:T(8,128)(2,1)S(1)} async-done(((bf16[32,32,768]{2,1,0:T(8,128)(2,1)}), bf16[32,32,768]{2,1,0:T(8,128)(2,1)S(1)}, u32[]{:S(2)}, u32[]{:S(2)}) %all-to-all-start.1) | async-done | bytes 1572896 | tf_op jit(solution)/shard_map/all_to_all | solution.py:442
  189.0 1.2 copy-done.2
  190.1 5.3 %shard_map.182 = (bf16[32,8192]{1,0:T(8,128)(2,1)}, bf16[32,8192]{1,0:T(8,128)(2,1)}, bf16[32,1024]{1,0:T(8,128)(2,1)}, bf16[32,1024]{1,0:T(8,128)(2,1)}) custom-call(bf16[32,32,768]{2,1,0:T(8,128)(2,1)} %copy-done.2), custom_call_target="tpu_custom_call" | custom-call | tf_op jit(solution)/shard_map/pallas_call | solution.py:102
  195.4 0.0 collective-permute-done.7.one_ref
  195.4 0.0 copy-start.6
  195.5 0.0 collective-permute-done.8.two_ref
  195.5 0.6 copy-done.6
  196.1 0.1 copy-done.7
  196.2 1.7 shard_map.186
  (24 shorter events, 0.1 us)
Async XLA Ops:
  2.3 14.7 %copy-start.3 = (bf16[32,2048]{1,0:T(8,128)(2,1)}, bf16[32,2048]{1,0:T(8,128)(2,1)S(1)}, u32[]{:S(2)}) copy-start(bf16[32,2048]{1,0:T(8,128)(2,1)S(1)} %constant_dynamic-update-slice_fusion.k0.v0) | copy-start | bytes 393220
  2.3 12.8 %collective-permute-start.5 = (bf16[32,2048]{1,0:T(8,128)(2,1)S(1)}, bf16[32,2048]{1,0:T(8,128)(2,1)S(1)}, u32[]{:S(2)}, u32[]{:S(2)}) collective-permute-start(bf16[32,2048]{1,0:T(8,128)(2,1)S(1)} %constant_dynamic-update-slice_fusion.k0.v0), channel_id=1, source_target_pairs={{0,64},{32,96},{64,128},{96,160},{128,192},{160,224},{1,65},{33,97... | collective-permute-start | bytes 393224 | tf_op jit(solution)/shard_map/ppermute | solution.py:438
  8.7 8.3 %collective-permute-start.6 = (bf16[32,2048]{1,0:T(8,128)(2,1)S(1)}, bf16[32,2048]{1,0:T(8,128)(2,1)S(1)}, u32[]{:S(2)}, u32[]{:S(2)}) collective-permute-start(bf16[32,2048]{1,0:T(8,128)(2,1)S(1)} %constant_dynamic-update-slice_fusion.k0.v0), channel_id=1, source_target_pairs={{0,32},{32,64},{64,96},{96,128},{128,160},{160,192},{192,224},{1,3... | collective-permute-start | bytes 393224 | tf_op jit(solution)/shard_map/ppermute | solution.py:438
  15.1 1.9 copy-start.4
  17.0 0.7 copy-start.5
  22.9 34.8 %all-to-all-start.2 = ((bf16[32,32,1024]{2,1,0:T(8,128)(2,1)}), bf16[32,32,1024]{2,1,0:T(8,128)(2,1)S(1)}, u32[]{:S(2)}, u32[]{:S(2)}) async-start(bf16[32,32,1024]{2,1,0:T(8,128)(2,1)} %shard_map.183), calls=%async_computation.2 | async-start | bytes 4194304 | tf_op jit(solution)/shard_map/all_to_all | solution.py:442
  35.5 28.4 %copy-start.13 = (s32[64]{0:T(128)S(1)}, s32[64]{0:T(128)}, u32[]{:S(2)}) copy-start(s32[64]{0:T(128)} %param.21) | copy-start | bytes 772
  57.7 1.3 copy-start.1
  59.0 29.9 %all-to-all-start = ((bf16[32,32,896]{2,1,0:T(8,128)(2,1)}), bf16[32,32,896]{2,1,0:T(8,128)(2,1)S(1)}, u32[]{:S(2)}, u32[]{:S(2)}) async-start(bf16[32,32,896]{2,1,0:T(8,128)(2,1)} %shard_map.179), calls=%async_computation | async-start | bytes 3670016 | tf_op jit(solution)/shard_map/all_to_all | solution.py:442
  64.4 0.6 copy-start.12
  88.9 1.2 copy-start
  88.9 6.0 %copy-start.14 = (f32[32]{0:T(128)S(1)}, f32[32]{0:T(128)}, u32[]{:S(2)}) copy-start(f32[32]{0:T(128)} %param.17) | copy-start | bytes 388
  88.9 6.0 %copy-start.15 = (f32[32]{0:T(128)S(1)}, f32[32]{0:T(128)}, u32[]{:S(2)}) copy-start(f32[32]{0:T(128)} %param.16) | copy-start | bytes 388
  90.2 45.8 %all-to-all-start.3 = ((bf16[32,32,1024]{2,1,0:T(8,128)(2,1)}), bf16[32,32,1024]{2,1,0:T(8,128)(2,1)}, u32[]{:S(2)}, u32[]{:S(2)}) async-start(bf16[32,32,1024]{2,1,0:T(8,128)(2,1)} %bitcast.24), calls=%async_computation.3 | async-start | bytes 4194304 | tf_op jit(solution)/shard_map/all_to_all | solution.py:442
  95.0 1.7 collective-permute-start
  102.3 14.6 %collective-permute-start.1 = (bf16[144,256]{1,0:T(8,128)(2,1)}, bf16[144,256]{1,0:T(8,128)(2,1)S(1)}, u32[]{:S(2)}, u32[]{:S(2)}) collective-permute-start(bf16[144,256]{1,0:T(8,128)(2,1)} %get-tuple-element.27), channel_id=1, source_target_pairs={{0,32},{32,64},{64,96},{96,128},{128,160},{160,192},{192,224},{1,3... | collective-permute-start | bytes 221192 | tf_op jit(solution)/shard_map/ppermute | solution.py:438
  106.7 10.2 %collective-permute-start.2 = (bf16[144,256]{1,0:T(8,128)(2,1)}, bf16[144,256]{1,0:T(8,128)(2,1)S(1)}, u32[]{:S(2)}, u32[]{:S(2)}) collective-permute-start(bf16[144,256]{1,0:T(8,128)(2,1)} %get-tuple-element.27), channel_id=1, source_target_pairs={{0,64},{32,96},{64,128},{96,160},{128,192},{160,224},{1,65},{33,97... | collective-permute-start | bytes 221192 | tf_op jit(solution)/shard_map/ppermute | solution.py:438
  110.4 6.5 %collective-permute-start.3 = (bf16[144,256]{1,0:T(8,128)(2,1)}, bf16[144,256]{1,0:T(8,128)(2,1)S(1)}, u32[]{:S(2)}, u32[]{:S(2)}) collective-permute-start(bf16[144,256]{1,0:T(8,128)(2,1)} %get-tuple-element.28), channel_id=1, source_target_pairs={{32,0},{64,32},{96,64},{128,96},{160,128},{192,160},{224,192},{33,... | collective-permute-start | bytes 221192 | tf_op jit(solution)/shard_map/ppermute | solution.py:438
  114.3 9.3 %collective-permute-start.4 = (bf16[144,256]{1,0:T(8,128)(2,1)}, bf16[144,256]{1,0:T(8,128)(2,1)S(1)}, u32[]{:S(2)}, u32[]{:S(2)}) collective-permute-start(bf16[144,256]{1,0:T(8,128)(2,1)} %get-tuple-element.28), channel_id=1, source_target_pairs={{64,0},{96,32},{128,64},{160,96},{192,128},{224,160},{65,1},{97,33... | collective-permute-start | bytes 221192 | tf_op jit(solution)/shard_map/ppermute | solution.py:438
  116.9 6.8 %copy-start.8 = (bf16[144,256]{1,0:T(8,128)(2,1)}, bf16[144,256]{1,0:T(8,128)(2,1)S(1)}, u32[]{:S(2)}) copy-start(bf16[144,256]{1,0:T(8,128)(2,1)S(1)} %collective-permute-done.1.f1) | copy-start | bytes 221188
  116.9 6.7 %copy-start.9 = (bf16[144,256]{1,0:T(8,128)(2,1)}, bf16[144,256]{1,0:T(8,128)(2,1)S(1)}, u32[]{:S(2)}) copy-start(bf16[144,256]{1,0:T(8,128)(2,1)S(1)} %collective-permute-done.2.f2) | copy-start | bytes 221188
  116.9 6.7 %copy-start.10 = (bf16[144,256]{1,0:T(8,128)(2,1)}, bf16[144,256]{1,0:T(8,128)(2,1)S(1)}, u32[]{:S(2)}) copy-start(bf16[144,256]{1,0:T(8,128)(2,1)S(1)} %collective-permute-done.3.b1) | copy-start | bytes 221188
  123.7 0.6 copy-start.11
  136.0 53.0 %all-to-all-start.1 = ((bf16[32,32,768]{2,1,0:T(8,128)(2,1)}), bf16[32,32,768]{2,1,0:T(8,128)(2,1)S(1)}, u32[]{:S(2)}, u32[]{:S(2)}) async-start(bf16[32,32,768]{2,1,0:T(8,128)(2,1)} %bitcast.26), calls=%async_computation.1 | async-start | bytes 3145728 | tf_op jit(solution)/shard_map/all_to_all | solution.py:442
  171.9 23.6 %collective-permute-start.7 = (bf16[32,2048]{1,0:T(8,128)(2,1)}, bf16[32,2048]{1,0:T(8,128)(2,1)S(1)}, u32[]{:S(2)}, u32[]{:S(2)}) collective-permute-start(bf16[32,2048]{1,0:T(8,128)(2,1)} %get-tuple-element.36), channel_id=1, source_target_pairs={{32,0},{64,32},{96,64},{128,96},{160,128},{192,160},{224,192},{33,... | collective-permute-start | bytes 393224 | tf_op jit(solution)/shard_map/ppermute | solution.py:438
  173.8 21.7 %collective-permute-start.8 = (bf16[32,2048]{1,0:T(8,128)(2,1)}, bf16[32,2048]{1,0:T(8,128)(2,1)S(1)}, u32[]{:S(2)}, u32[]{:S(2)}) collective-permute-start(bf16[32,2048]{1,0:T(8,128)(2,1)} %get-tuple-element.37), channel_id=1, source_target_pairs={{64,0},{96,32},{128,64},{160,96},{192,128},{224,160},{65,1},{97,33... | collective-permute-start | bytes 393224 | tf_op jit(solution)/shard_map/ppermute | solution.py:438
  189.0 1.2 copy-start.2
  195.4 0.6 copy-start.6
  195.5 0.7 copy-start.7
where the time goes:
time: 200 us; the launch traced here: 198 us
  starting transfers between devices  75.1 us (38%)
  Pallas kernels  59.3 us (30%)
  waiting for transfers between devices  51.8 us (26%)
  local copies, waits for them, and re-layouts  8.88 us (4%)
    all_to_all x4, starting transfers between devices, exchange(): return lax.all_to_all(block, GROUP, split_axis=0, concat_axis=0, tiled=True)  47.5 us
    all_to_all x4, waiting for transfers between devices, exchange(): return lax.all_to_all(block, GROUP, split_axis=0, concat_axis=0, tiled=True)  39.7 us
    ppermute x8, starting transfers between devices, shifted(): return lax.ppermute(block, 'z', route)  27 us
    pallas_call x1, Pallas kernels, do_attention(): pl.pallas_call(attention_kernel, in_specs=[smem(), vmem(), vmem()], out_s...  19.5 us
    ppermute x8, waiting for transfers between devices, shifted(): return lax.ppermute(block, 'z', route)  12.1 us
    pallas_call x1, Pallas kernels, do_mixer(): pl.pallas_call(mixer_kernel, in_specs=[smem()] * 3 + [vmem()] * 9, out_sp...  11.7 us
    unnamed x33, local copies, waits for them, and re-layouts  6.58 us
    pallas_call x1, Pallas kernels, do_unpack_attention(): pl.pallas_call(unpack_attention, grid=(8,), in_specs=[pl.BlockSpec((4, RO...  5.41 us
  transfers between devices with their start and end apart: 13, of which 6 were waited for; matrix products, arithmetic and copies ran while one was open for 2% of the time, Pallas kernels for 26%

commit v1 on v0

--- a/solution.py
+++ b/solution.py
@@ -18,10 +18,12 @@
 STATE = 128
 LANES = 128
 SCALE = 128 ** (-0.5)
-TQ = 256
+TQ = 512
 TK = 512
+PAD = 0
+UNROLL = 2
 NEG = -1e30
-VMEM = 60 * 1024 * 1024
+VMEM = 36 * 1024 * 1024
 NN = (((1,), (0,)), ((), ()))
 NT = (((1,), (1,)), ((), ()))
 TN = (((0,), (0,)), ((), ()))
@@ -43,67 +45,72 @@
     return pl.BlockSpec(memory_space=pltpu.VMEM)
 
 
+def places():
+    for core in range(2):
+        for tp in range(4):
+            yield core, tp // 2, core * 4 + tp, (tp // 2) * 4 + core * 2 + tp % 2
+
+
 def pack_mixer(x_ref, gy_ref, b_ref, c_ref, dt_ref, out_ref):
-    for t in range(4):
-        out_ref[t, :, 0:256] = x_ref[:, t * 256 : t * 256 + 256]
-        out_ref[t, :, 256:512] = gy_ref[:, t * 256 : t * 256 + 256]
-        out_ref[t, :, 512:640] = b_ref[...]
-        out_ref[t, :, 640:768] = c_ref[...]
-        out_ref[t, :, 768:896] = dt_ref[...]
-
-
-def pack_attention(q_ref, ga_ref, k2, v2, k1, v1, k0, v0, out_ref):
-    for t in range(4):
-        out_ref[t, :, 0:128] = q_ref[:, t * 128 : t * 128 + 128]
-        out_ref[t, :, 128:256] = ga_ref[:, t * 128 : t * 128 + 128]
-        for n, ref in enumerate((k2, v2, k1, v1, k0, v0)):
-            out_ref[t, :, 256 + n * 128 : 384 + n * 128] = ref[...]
+    for core, side, at, slot in places():
+        out_ref[at, :, 0:256] = x_ref[:, slot * 256 : slot * 256 + 256]
+        out_ref[at, :, 256:512] = gy_ref[:, slot * 256 : slot * 256 + 256]
+        out_ref[at, :, 512:640] = b_ref[:, side * 128 : side * 128 + 128]
+        out_ref[at, :, 640:768] = c_ref[:, side * 128 : side * 128 + 128]
+        out_ref[at, :, 768:896] = dt_ref[...]
+
+
+def pack_attention(q_ref, ga_ref, k_ref, v_ref, out_ref):
+    for core, side, at, slot in places():
+        out_ref[at, :, 0:128] = q_ref[:, slot * 128 : slot * 128 + 128]
+        out_ref[at, :, 128:256] = ga_ref[:, slot * 128 : slot * 128 + 128]
+        out_ref[at, :, 256:384] = (k_ref, v_ref)[core][:, side * 128 : side * 128 + 128]
 
 
 def wide(width, place=0):
-    return pl.BlockSpec((ROWS, width), lambda g: (0, g + place))
+    return pl.BlockSpec((ROWS, width), lambda y: (0, y + place))
 
 
 def do_pack_mixer(xs, gy, bs, cs, dts):
     return pl.pallas_call(
         pack_mixer,
-        grid=(8,),
-        in_specs=[wide(1024), wide(1024), wide(128), wide(128), pl.BlockSpec((ROWS, 128), lambda g: (0, 0))],
-        out_specs=pl.BlockSpec((4, ROWS, 896), lambda g: (g, 0, 0)),
+        grid=(4,),
+        in_specs=[wide(2048), wide(2048), wide(256), wide(256), pl.BlockSpec((ROWS, 128), lambda y: (0, 0))],
+        out_specs=pl.BlockSpec((8, ROWS, 896), lambda y: (y, 0, 0)),
         out_shape=jax.ShapeDtypeStruct((32, ROWS, 896), BF),
         compiler_params=params(),
     )(xs, gy, bs, cs, dts)
 
 
-def do_pack_attention(q, ga, kv2, kv1, kv0):
+def do_pack_attention(q, ga, keys, values):
     return pl.pallas_call(
         pack_attention,
-        grid=(8,),
-        in_specs=[wide(512), wide(512)] + [wide(128), wide(128, 8)] * 3,
-        out_specs=pl.BlockSpec((4, ROWS, 1024), lambda g: (g, 0, 0)),
-        out_shape=jax.ShapeDtypeStruct((32, ROWS, 1024), BF),
-        compiler_params=params(),
-    )(q, ga, kv2, kv2, kv1, kv1, kv0, kv0)
+        grid=(4,),
+        in_specs=[wide(1024), wide(1024), wide(256), wide(256)],
+        out_specs=pl.BlockSpec((8, ROWS, 384), lambda y: (y, 0, 0)),
+        out_shape=jax.ShapeDtypeStruct((32, ROWS, 384), BF),
+        compiler_params=params(),
+    )(q, ga, keys, values)
 
 
 def unpack_mixer(in_ref, y_ref, gx_ref, gb_ref, gc_ref):
-    gb = jnp.zeros((ROWS, 128), F32)
-    gc = jnp.zeros((ROWS, 128), F32)
-    for t in range(4):
-        y_ref[:, t * 256 : t * 256 + 256] = in_ref[t, :, 0:256]
-        gx_ref[:, t * 256 : t * 256 + 256] = in_ref[t, :, 256:512]
-        gb = gb + in_ref[t, :, 512:640].astype(F32)
-        gc = gc + in_ref[t, :, 640:768].astype(F32)
-    gb_ref[...] = gb.astype(BF)
-    gc_ref[...] = gc.astype(BF)
+    gb = [jnp.zeros((ROWS, 128), F32)] * 2
+    gc = [jnp.zeros((ROWS, 128), F32)] * 2
+    for core, side, at, slot in places():
+        y_ref[:, slot * 256 : slot * 256 + 256] = in_ref[at, :, 0:256]
+        gx_ref[:, slot * 256 : slot * 256 + 256] = in_ref[at, :, 256:512]
+        gb[side] = gb[side] + in_ref[at, :, 512:640].astype(F32)
+        gc[side] = gc[side] + in_ref[at, :, 640:768].astype(F32)
+    gb_ref[...] = jnp.concatenate(gb, axis=1).astype(BF)
+    gc_ref[...] = jnp.concatenate(gc, axis=1).astype(BF)
 
 
 def do_unpack_mixer(got):
     return pl.pallas_call(
         unpack_mixer,
-        grid=(8,),
-        in_specs=[pl.BlockSpec((4, ROWS, 768), lambda g: (g, 0, 0))],
-        out_specs=[wide(1024), wide(1024), wide(128), wide(128)],
+        grid=(4,),
+        in_specs=[pl.BlockSpec((8, ROWS, 768), lambda y: (y, 0, 0))],
+        out_specs=[wide(2048), wide(2048), wide(256), wide(256)],
         out_shape=[
             jax.ShapeDtypeStruct((ROWS, 8192), BF),
             jax.ShapeDtypeStruct((ROWS, 8192), BF),
@@ -114,23 +121,27 @@
     )(got)
 
 
-def unpack_attention(in_ref, att_ref, gq_ref, kv2_ref, kv1_ref, kv0_ref):
-    for t in range(4):
-        att_ref[:, t * 128 : t * 128 + 128] = in_ref[t, :, 0:128]
-        gq_ref[:, t * 128 : t * 128 + 128] = in_ref[t, :, 128:256]
-    for n, ref in enumerate((kv2_ref, kv1_ref, kv0_ref)):
-        total = in_ref[0, :, 256 + n * 256 : 512 + n * 256].astype(F32)
-        for t in range(1, 4):
-            total = total + in_ref[t, :, 256 + n * 256 : 512 + n * 256].astype(F32)
-        ref[...] = total.astype(ref.dtype)
+def unpack_attention(in_ref, att_ref, gq_ref, two_ref, one_ref, own_ref):
+    refs = (two_ref, one_ref, own_ref)
+    totals = {}
+    for core, side, at, slot in places():
+        att_ref[:, slot * 128 : slot * 128 + 128] = in_ref[at, :, 0:128]
+        gq_ref[:, slot * 128 : slot * 128 + 128] = in_ref[at, :, 128:256]
+        for n in range(3):
+            part = in_ref[at, :, 256 + n * 128 : 384 + n * 128].astype(F32)
+            where = (n, core, side)
+            totals[where] = totals[where] + part if where in totals else part
+    for (n, core, side), total in totals.items():
+        col = core * 256 + side * 128
+        refs[n][:, col : col + 128] = total.astype(refs[n].dtype)
 
 
 def do_unpack_attention(got):
     return pl.pallas_call(
         unpack_attention,
-        grid=(8,),
-        in_specs=[pl.BlockSpec((4, ROWS, 1024), lambda g: (g, 0, 0))],
-        out_specs=[wide(512), wide(512), wide(256), wide(256), wide(256)],
+        grid=(4,),
+        in_specs=[pl.BlockSpec((8, ROWS, 640), lambda y: (y, 0, 0))],
+        out_specs=[wide(1024), wide(1024), wide(512), wide(512), wide(512)],
         out_shape=[
             jax.ShapeDtypeStruct((ROWS, 4096), BF),
             jax.ShapeDtypeStruct((ROWS, 4096), BF),
@@ -143,11 +154,11 @@
 
 
 def add_kv(own_ref, one_ref, two_ref, gk_ref, gv_ref):
-    for g in range(8):
-        at = slice(g * 256, g * 256 + 256)
+    for y in range(4):
+        at = slice(y * 512, y * 512 + 512)
         total = (own_ref[:, at] + one_ref[:, at].astype(F32) + two_ref[:, at].astype(F32)).astype(BF)
-        gk_ref[:, g * 128 : g * 128 + 128] = total[:, 0:128]
-        gv_ref[:, g * 128 : g * 128 + 128] = total[:, 128:256]
+        gk_ref[:, y * 256 : y * 256 + 256] = total[:, 0:256]
+        gv_ref[:, y * 256 : y * 256 + 256] = total[:, 256:512]
 
 
 def do_add_kv(own, one, two):
@@ -158,6 +169,24 @@
         out_shape=[jax.ShapeDtypeStruct((ROWS, 1024), BF)] * 2,
         compiler_params=params(),
     )(own, one, two)
+
+
+def pack_back(att_ref, keep_ref, come_ref, out_ref):
+    out_ref[:, 0:256] = att_ref[...]
+    for n in range(3):
+        rows = slice(n * SUPER, n * SUPER + SUPER)
+        total = keep_ref[rows, :].astype(F32) + come_ref[rows, :].astype(F32)
+        out_ref[:, 256 + n * 128 : 384 + n * 128] = total.astype(BF)
+
+
+def do_pack_back(att, keep, come):
+    return pl.pallas_call(
+        pack_back,
+        in_specs=[vmem()] * 3,
+        out_specs=vmem(),
+        out_shape=jax.ShapeDtypeStruct((SUPER, 640), BF),
+        compiler_params=params(),
+    )(att, keep, come)
 
 
 def lane_row(values, width):
@@ -329,7 +358,7 @@
         out_ref[rows, 640:768] = gc.astype(BF)
         return 0
 
-    lax.fori_loop(0, BLOCKS, one, 0)
+    lax.fori_loop(0, BLOCKS, one, 0, unroll=UNROLL)
 
 
 def do_mixer(info, rates, skips, got, ends, inc, back, factor, f1, f2, b1, b2):
@@ -342,94 +371,146 @@
     )(info, rates, skips, got, ends, inc, back, factor, f1, f2, b1, b2)
 
 
-def attention_kernel(starts, in_ref, start_ref, out_ref, kt_ref, vt_ref, s_ref, acc_ref):
-    tiles = 3 * SUPER // TK
-    lowest = starts[0] // TK
-
-    def key_at(t):
-        rows = pl.ds(pl.multiple_of((t % 2) * TK, TK), TK)
-        return rows, pl.multiple_of(256 + (t // 2) * 256, 256)
-
-    def turn(t, _):
-        rows, col = key_at(t)
-        kt_ref[t] = in_ref[rows, pl.ds(col, 128)].T
-        vt_ref[t] = in_ref[rows, pl.ds(col + 128, 128)].T
-        return 0
-
-    lax.fori_loop(lowest, tiles, turn, 0)
-    acc_ref[...] = jnp.zeros_like(acc_ref)
-
-    def one(i, _):
-        rows = pl.ds(pl.multiple_of(i * TQ, TQ), TQ)
-        q = in_ref[rows, 0:128]
-        ga = in_ref[rows, 128:256]
-        begin = start_ref[pl.ds(i, 1), :]
-        here = 2 * SUPER + i * TQ + lax.broadcasted_iota(jnp.int32, (1, TQ), 1)
-        low = starts[i * TQ] // TK
-        high = (2 * SUPER + i * TQ + TQ - 1) // TK + 1
-
-        def score(t, peak):
-            krows, col = key_at(t)
-            s = dot(in_ref[krows, pl.ds(col, 128)], q, NT) * SCALE
-            at = t * TK + lax.broadcasted_iota(jnp.int32, (TK, TQ), 0)
-            s = jnp.where((at >= begin) & (at <= here), s, NEG)
-            s_ref[t] = s
-            return jnp.maximum(peak, jnp.max(s.reshape(TK // 8, 8, TQ), axis=0))
-
-        peak = lax.fori_loop(low, high, score, jnp.full((8, TQ), NEG, F32))
-        peak = jnp.max(peak, axis=0, keepdims=True)
-
-        def weigh(t, carry):
-            total, att = carry
-            p = jnp.exp(s_ref[t] - peak)
-            s_ref[t] = p
-            total = total + jnp.sum(p.reshape(TK // 8, 8, TQ), axis=0)
-            return total, att + dot(vt_ref[t], p.astype(BF))
-
-        total, att = lax.fori_loop(
-            low, high, weigh, (jnp.zeros((8, TQ), F32), jnp.zeros((128, TQ), F32))
-        )
+def attention_kernel(
+    core, starts, in_ref, own1, own2, oth0, oth1, oth2, start_ref, out_ref, keep_ref, send_ref,
+    k_ref, v_ref, kt_ref, vt_ref, near_ref, far_ref, peak_ref, gk_ref, gv_ref
+):
+    count = SUPER // TQ
+    lowest = starts[0] - TK + 1
+    gk_ref[...] = jnp.zeros_like(gk_ref)
+    gv_ref[...] = jnp.zeros_like(gv_ref)
+    for n in range(3):
+        rows = slice(PAD + n * SUPER, PAD + n * SUPER + SUPER)
+        own = (own2, own1, in_ref.at[:, 256:384])[n]
+        other = (oth2, oth1, oth0)[n]
+
+        @pl.when((lowest < (n + 1) * SUPER) & (core[0] == 0))
+        def _():
+            k_ref[rows, :] = own[...]
+            v_ref[rows, :] = other[...]
+
+        @pl.when((lowest < (n + 1) * SUPER) & (core[0] != 0))
+        def _():
+            k_ref[rows, :] = other[...]
+            v_ref[rows, :] = own[...]
+
+        @pl.when(lowest < (n + 1) * SUPER)
+        def _():
+            kt_ref[:, rows] = k_ref[rows, :].T
+            vt_ref[:, rows] = v_ref[rows, :].T
+
+    def tile_sum(p):
+        return jnp.sum(p.reshape(p.shape[0] // 8, 8, TQ), axis=0)
+
+    at = lax.broadcasted_iota(jnp.int32, (TQ, TQ), 0)
+    here = lax.broadcasted_iota(jnp.int32, (TQ, TQ), 1)
+    far_at = lax.broadcasted_iota(jnp.int32, (TK, TQ), 0)
+    q_rows = [slice(i * TQ, i * TQ + TQ) for i in range(count)]
+    diag = [2 * SUPER + i * TQ for i in range(count)]
+    near = [slice(PAD + diag[i], PAD + diag[i] + TQ) for i in range(count)]
+    begins = [start_ref[i : i + 1, :] for i in range(count)]
+    many = [(jnp.maximum(diag[i] - starts[i * TQ], 0) + TK - 1) // TK for i in range(count)]
+
+    carries = []
+    for i in range(count):
+        q = in_ref[q_rows[i], 0:128]
+        s = dot(k_ref[near[i], :], q, NT)
+        s = jnp.where((at + diag[i] >= begins[i]) & (at <= here), s, NEG)
+        peak = jnp.max(s, axis=0, keepdims=True)
+        p = jnp.exp((s - peak) * SCALE)
+        near_ref[i] = p
+        peak_ref[i, 4:5, :] = peak
+        carries.append((peak, tile_sum(p), dot(vt_ref[:, near[i]], p.astype(BF))))
+
+    for i in range(count):
+        q = in_ref[q_rows[i], 0:128]
+
+        def forward(t, carry):
+            peak, total, att = carry
+            base = diag[i] - TK * (t + 1)
+            rows = pl.ds(pl.multiple_of(PAD + base, TQ), TK)
+            s = dot(k_ref[rows, :], q, NT)
+            s = jnp.where(far_at >= begins[i] - base, s, NEG)
+            top = jnp.maximum(peak, jnp.max(s, axis=0, keepdims=True))
+            alpha = jnp.exp((peak - top) * SCALE)
+            p = jnp.exp((s - top) * SCALE)
+            far_ref[i, t] = p
+            peak_ref[i, pl.ds(t, 1), :] = top
+            att = att * alpha + dot(vt_ref[:, rows], p.astype(BF))
+            return top, total * alpha + tile_sum(p), att
+
+        carries[i] = lax.fori_loop(0, many[i], forward, carries[i])
+
+    rest = []
+    for i in range(count):
+        peak, total, att = carries[i]
+        q = in_ref[q_rows[i], 0:128]
+        ga = in_ref[q_rows[i], 128:256]
         inverse = 1.0 / jnp.sum(total, axis=0, keepdims=True)
-        att = (att * inverse).T.astype(BF)
-        out_ref[rows, 0:128] = att
-        delta = jnp.sum((ga.astype(F32) * att.astype(F32)).T, axis=0, keepdims=True)
-
-        def grads(t, gq):
-            krows, col = key_at(t)
-            probs = s_ref[t] * inverse
-            dp = dot(in_ref[krows, pl.ds(col + 128, 128)], ga, NT)
-            ds = (probs * (dp - delta)).astype(BF)
-            acc_ref[t, :, 0:128] += dot(ds, q)
-            acc_ref[t, :, 128:256] += dot(probs.astype(BF), ga)
-            return gq + dot(kt_ref[t], ds)
-
-        gq = lax.fori_loop(low, high, grads, jnp.zeros((128, TQ), F32))
-        out_ref[rows, 128:256] = (gq * SCALE).T.astype(BF)
-        return 0
-
-    lax.fori_loop(0, SUPER // TQ, one, 0)
-    for t in range(tiles):
-        rows = slice((t % 2) * TK, (t % 2) * TK + TK)
-        col = 256 + (t // 2) * 256
-        out_ref[rows, col : col + 128] = (acc_ref[t, :, 0:128] * SCALE).astype(BF)
-        out_ref[rows, col + 128 : col + 256] = acc_ref[t, :, 128:256].astype(BF)
-
-
-def do_attention(starts, got):
-    tiles = 3 * SUPER // TK
+        att = (att * inverse).astype(BF)
+        out_ref[q_rows[i], 0:128] = att.T
+        delta = jnp.sum(ga.T.astype(F32) * att.astype(F32), axis=0, keepdims=True)
+        probs = near_ref[i] * (jnp.exp((peak_ref[i, 4:5, :] - peak) * SCALE) * inverse)
+        ds = (probs * (dot(v_ref[near[i], :], ga, NT) - delta)).astype(BF)
+        gk_ref[near[i], :] += dot(ds, q)
+        gv_ref[near[i], :] += dot(probs.astype(BF), ga)
+        rest.append((peak, inverse, delta, dot(kt_ref[:, near[i]], ds)))
+
+    for i in range(count):
+        peak, inverse, delta, gq = rest[i]
+        q = in_ref[q_rows[i], 0:128]
+        ga = in_ref[q_rows[i], 128:256]
+
+        def backward(t, gq):
+            rows = pl.ds(pl.multiple_of(PAD + diag[i] - TK * (t + 1), TQ), TK)
+            factor = jnp.exp((peak_ref[i, pl.ds(t, 1), :] - peak) * SCALE) * inverse
+            probs = far_ref[i, t] * factor
+            ds = (probs * (dot(v_ref[rows, :], ga, NT) - delta)).astype(BF)
+            gk_ref[rows, :] += dot(ds, q)
+            gv_ref[rows, :] += dot(probs.astype(BF), ga)
+            return gq + dot(kt_ref[:, rows], ds)
+
+        gq = lax.fori_loop(0, many[i], backward, gq)
+        out_ref[q_rows[i], 128:256] = (gq * SCALE).astype(BF).T
+
+    def store(k_out, v_out):
+        k_out[...] = (gk_ref[PAD:, :] * SCALE).astype(BF)
+        v_out[...] = gv_ref[PAD:, :].astype(BF)
+
+    @pl.when(core[0] == 0)
+    def _():
+        store(keep_ref, send_ref)
+
+    @pl.when(core[0] != 0)
+    def _():
+        store(send_ref, keep_ref)
+
+
+def do_attention(core, starts, got, own1, own2, oth0, oth1, oth2):
+    span = PAD + 3 * SUPER
+    count = SUPER // TQ
     return pl.pallas_call(
         attention_kernel,
-        in_specs=[smem(), vmem(), vmem()],
-        out_specs=vmem(),
-        out_shape=jax.ShapeDtypeStruct((SUPER, 1024), BF),
+        in_specs=[smem(), smem()] + [vmem()] * 7,
+        out_specs=[vmem()] * 3,
+        out_shape=[
+            jax.ShapeDtypeStruct((SUPER, 256), BF),
+            jax.ShapeDtypeStruct((3 * SUPER, 128), BF),
+            jax.ShapeDtypeStruct((3 * SUPER, 128), BF),
+        ],
         scratch_shapes=[
-            pltpu.VMEM((tiles, 128, TK), BF),
-            pltpu.VMEM((tiles, 128, TK), BF),
-            pltpu.VMEM((tiles, TK, TQ), F32),
-            pltpu.VMEM((tiles, TK, 256), F32),
+            pltpu.VMEM((span, 128), BF),
+            pltpu.VMEM((span, 128), BF),
+            pltpu.VMEM((128, span), BF),
+            pltpu.VMEM((128, span), BF),
+            pltpu.VMEM((count, TQ, TQ), F32),
+            pltpu.VMEM((count, 4, TK, TQ), F32),
+            pltpu.VMEM((count, 8, TQ), F32),
+            pltpu.VMEM((span, 128), F32),
+            pltpu.VMEM((span, 128), F32),
         ],
         compiler_params=params(),
-    )(starts, got, starts.reshape(SUPER // TQ, TQ))
+    )(core, starts, got, own1, own2, oth0, oth1, oth2, starts.reshape(SUPER // TQ, TQ))
 
 
 def shifted(block, distance):
@@ -442,20 +523,25 @@
     return lax.all_to_all(block, GROUP, split_axis=0, concat_axis=0, tiled=True)
 
 
+def swapped(block):
+    return lax.ppermute(block, "core", [(0, 1), (1, 0)])
+
+
 def per_device(xs, dts, bs, cs, rates, skips, queries, keys, values, lengths, grad_y, grad_attn):
     z, y, core, tp = (lax.axis_index(a) for a in ("z", "y", "core", "tp"))
-    device = (y * 2 + core) * 4 + tp
-
-    kv0 = jnp.concatenate([keys, values], axis=1)
-    kv1 = shifted(kv0, 1)
-    kv2 = shifted(kv0, 2)
+    inside = (tp // 2) * 4 + core * 2 + tp % 2
+    device = y * 8 + inside
+
+    packed_a = do_pack_attention(queries, grad_attn, keys, values)
+    packed_a, xs, rates = lax.optimization_barrier((packed_a, xs, rates))
     side = lax.axis_size("tp")
     both = lax.ppermute(
         jnp.stack([rates, skips]),
         ("y", "tp"),
         [(a * side + b, b * side + a) for a in range(side) for b in range(side)],
     )
-    mine = lax.dynamic_slice_in_dim(both, core * 16 + tp * HEADS, HEADS, 1)
+    packed_m = do_pack_mixer(xs, grad_y, bs, cs, dts)
+    mine = lax.dynamic_slice_in_dim(both, inside * HEADS, HEADS, 1)
     my_rates, my_skips = mine[0], mine[1]
 
     ends = jnp.cumsum(lengths)
@@ -482,23 +568,34 @@
     )
     local_stops = (stops.reshape(BLOCKS, BLOCK) - block_at[:, None]).astype(jnp.int32)
 
-    got = exchange(do_pack_mixer(xs, grad_y, bs, cs, dts)).reshape(SUPER, 896)
+    got_a = exchange(packed_a)
+    packed_m, got_a = lax.optimization_barrier((packed_m, got_a))
+    got_a = got_a.reshape(SUPER, 384)
+    own0 = got_a[:, 256:384]
+    own1, own2 = shifted(own0, 1), shifted(own0, 2)
+    got = exchange(packed_m)
+    att, keep, send = do_attention(
+        jnp.full((1,), core, jnp.int32),
+        (starts - (base - 2 * SUPER)).astype(jnp.int32),
+        got_a, own1, own2, swapped(own0), swapped(own1), swapped(own2),
+    )
+    send, got = lax.optimization_barrier((send, got))
+    got = got.reshape(SUPER, 896)
+    packed_b = do_pack_back(att, keep, swapped(send))
+    out_a = exchange(packed_b.reshape(32, ROWS, 640))
+
     inc, back, factor, send_f, send_b = do_state(info, my_rates, got)
     f1, f2 = shifted(send_f, 1), shifted(send_f, 2)
     b1, b2 = shifted(send_b, -1), shifted(send_b, -2)
-
-    got_a = exchange(do_pack_attention(queries, grad_attn, kv2, kv1, kv0)).reshape(SUPER, 1024)
-    attended = do_attention((starts - (base - 2 * SUPER)).astype(jnp.int32), got_a)
-    out_a = exchange(attended.reshape(32, ROWS, 1024))
-    att, gq, p2, p1, p0 = do_unpack_attention(out_a)
-    r1, r2 = shifted(p1, -1), shifted(p2, -2)
-
     mixed = do_mixer(
         info, my_rates, my_skips, got, local_stops, inc, back, factor, f1, f2, b1, b2
     )
+    mixed, out_a = lax.optimization_barrier((mixed, out_a))
     out_m = exchange(mixed.reshape(32, ROWS, 768))
+    att, gq, p2, p1, p0 = do_unpack_attention(out_a)
+    r1, r2 = shifted(p1, -1), shifted(p2, -2)
+    gk, gv = do_add_kv(p0, r1, r2)
     y_out, gx, gb, gc = do_unpack_mixer(out_m)
-    gk, gv = do_add_kv(p0, r1, r2)
     return y_out, gx, gb, gc, att, gq, gk, gv
 
 

time: 200 us -> 154 us (0.77)
  Pallas kernels: 59.3 us -> 25.8 us
  starting transfers between devices: 75.1 us -> 59.2 us
  local copies, waits for them, and re-layouts: 8.88 us -> 15.7 us
  waiting for transfers between devices: 51.8 us -> 48.3 us
    pallas_call x5 -> x6, Pallas kernels: 40.8 us -> 12.7 us  [the longest x1 7.52 us: do_attention(): pl.pallas_call(attention_kernel, in_specs=[smem(), smem()] + [vmem()] * 7...]
    all_to_all x4, waiting for transfers between devices: 39.7 us -> 16.5 us  [exchange(): return lax.all_to_all(block, GROUP, split_axis=0, concat_axis=0, tiled=True)]
    all_to_all x4, starting transfers between devices: 47.5 us -> 27.2 us  [exchange(): return lax.all_to_all(block, GROUP, split_axis=0, concat_axis=0, tiled=True)]
    ppermute x8, waiting for transfers between devices: 12.1 us -> 30.4 us  [shifted(): return lax.ppermute(block, 'z', route)]
    unnamed x33 -> x46, local copies, waits for them, and re-layouts: 6.58 us -> 14.7 us
    ppermute x8, starting transfers between devices: 27 us -> 30.8 us  [shifted(): return lax.ppermute(block, 'z', route)]
    pallas_call x1, Pallas kernels: 5.06 us -> 2.81 us  [do_state(): pl.pallas_call(state_kernel, in_specs=[smem(), smem(), vmem()], out_specs...]
    pallas_call x1, Pallas kernels: 11.7 us -> 9.56 us  [do_mixer(): pl.pallas_call(mixer_kernel, in_specs=[smem()] * 3 + [vmem()] * 9, out_sp...]
  transfers between devices with their start and end apart: 13 -> 17, of which waited for: 6 -> 9; matrix products, arithmetic and copies ran while one was open for 2% -> 1% of each run, Pallas kernels for 26% -> 15%
where the time goes in v1:
time: 154 us; the launch traced here: 151 us
  starting transfers between devices  59.2 us (38%)
  waiting for transfers between devices  48.3 us (31%)
  Pallas kernels  25.8 us (17%)
  local copies, waits for them, and re-layouts  15.7 us (10%)
    ppermute x8, starting transfers between devices, shifted(): return lax.ppermute(block, 'z', route)  30.8 us
    ppermute x8, waiting for transfers between devices, shifted(): return lax.ppermute(block, 'z', route)  30.4 us
    all_to_all x4, starting transfers between devices, exchange(): return lax.all_to_all(block, GROUP, split_axis=0, concat_axis=0, tiled=True)  27.2 us
    all_to_all x4, waiting for transfers between devices, exchange(): return lax.all_to_all(block, GROUP, split_axis=0, concat_axis=0, tiled=True)  16.5 us
    unnamed x46, local copies, waits for them, and re-layouts  14.7 us
    pallas_call x1, Pallas kernels, do_mixer(): pl.pallas_call(mixer_kernel, in_specs=[smem()] * 3 + [vmem()] * 9, out_sp...  9.56 us
    pallas_call x1, Pallas kernels, do_attention(): pl.pallas_call(attention_kernel, in_specs=[smem(), smem()] + [vmem()] * 7...  7.52 us
  transfers between devices with their start and end apart: 17, of which 9 were waited for; matrix products, arithmetic and copies ran while one was open for 1% of the time, Pallas kernels for 15%

profile of v1, /device:TPU:64, one launch (start us, length us, event | category | flops | bytes accessed | tf_op | source)
XLA Modules:
  0.0 150.8 jit_solution(4740956659701027609)
XLA Ops:
  0.7 1.0 copy-done.12
  1.7 0.9 copy-done.13
  2.6 0.8 copy-done.14
  3.4 0.8 copy-done.15
  4.3 1.6 %shard_map.179 = bf16[32,32,384]{2,1,0:T(8,128)(2,1)} custom-call(bf16[32,4096]{1,0:T(8,128)(2,1)S(1)} %copy-done.12, bf16[32,4096]{1,0:T(8,128)(2,1)S(1)} %copy-done.13, bf16[32,1024]{1,0:T(8,128)(2,1)S(1)} %copy-done.14, bf16[32,1024]{1,0:T(8,128)(2,1)S(1)} %copy-done.15), custom_call_target="tpu_custom_call" | custom-call | tf_op jit(solution)/shard_map/pallas_call | solution.py:86
  5.9 7.3 %all-to-all-start = ((bf16[32,32,384]{2,1,0:T(8,128)(2,1)}), bf16[32,32,384]{2,1,0:T(8,128)(2,1)S(1)}, u32[]{:S(2)}, u32[]{:S(2)}) async-start(bf16[32,32,384]{2,1,0:T(8,128)(2,1)} %shard_map.179), calls=%async_computation | async-start | bytes 1572864 | tf_op jit(solution)/shard_map/all_to_all | solution.py:523
  13.2 0.0 copy-start.3
  13.3 1.0 copy-done.3
  14.3 0.4 shard_map.180
  14.7 1.2 copy-done
  15.9 11.7 %all-to-all-done = bf16[32,32,384]{2,1,0:T(8,128)(2,1)S(1)} async-done(((bf16[32,32,384]{2,1,0:T(8,128)(2,1)}), bf16[32,32,384]{2,1,0:T(8,128)(2,1)S(1)}, u32[]{:S(2)}, u32[]{:S(2)}) %all-to-all-start) | async-done | bytes 786464 | tf_op jit(solution)/shard_map/all_to_all | solution.py:523
  27.6 4.0 %all-to-all-start.1 = ((bf16[32,32,896]{2,1,0:T(8,128)(2,1)}), bf16[32,32,896]{2,1,0:T(8,128)(2,1)S(1)}, u32[]{:S(2)}, u32[]{:S(2)}) async-start(bf16[32,32,896]{2,1,0:T(8,128)(2,1)} %copy-done), calls=%async_computation.1 | async-start | bytes 3670016 | tf_op jit(solution)/shard_map/all_to_all | solution.py:523
  31.7 0.0 copy-start.22
  31.7 0.7 slice.16
  32.4 6.4 %collective-permute-start.2 = (bf16[1024,128]{1,0:T(8,128)(2,1)}, bf16[1024,128]{1,0:T(8,128)(2,1)S(1)}, u32[]{:S(2)}, u32[]{:S(2)}) collective-permute-start(bf16[1024,128]{1,0:T(8,128)(2,1)} %slice.16), channel_id=1, source_target_pairs={{0,64},{32,96},{64,128},{96,160},{128,192},{160,224},{1,65},{33,97... | collective-permute-start | bytes 786440 | tf_op jit(solution)/shard_map/ppermute | solution.py:519
  38.8 2.9 %collective-permute-start.1 = (bf16[1024,128]{1,0:T(8,128)(2,1)}, bf16[1024,128]{1,0:T(8,128)(2,1)S(1)}, u32[]{:S(2)}, u32[]{:S(2)}) collective-permute-start(bf16[1024,128]{1,0:T(8,128)(2,1)} %slice.16), channel_id=1, source_target_pairs={{0,32},{32,64},{64,96},{96,128},{128,160},{160,192},{192,224},{1,3... | collective-permute-start | bytes 786440 | tf_op jit(solution)/shard_map/ppermute | solution.py:519
  41.8 0.1 copy.22
  41.9 0.1 reduce-window.8
  41.9 0.1 reduce
  42.1 0.1 collective-permute-start.3
  42.2 9.2 %collective-permute-done.2.own2 = bf16[1024,128]{1,0:T(8,128)(2,1)S(1)} collective-permute-done((bf16[1024,128]{1,0:T(8,128)(2,1)}, bf16[1024,128]{1,0:T(8,128)(2,1)S(1)}, u32[]{:S(2)}, u32[]{:S(2)}) %collective-permute-start.2) | collective-permute-done | bytes 262176 | tf_op jit(solution)/shard_map/ppermute | solution.py:519
  51.4 0.7 copy-done.6
  52.1 4.3 %collective-permute-done.1.own1 = bf16[1024,128]{1,0:T(8,128)(2,1)S(1)} collective-permute-done((bf16[1024,128]{1,0:T(8,128)(2,1)}, bf16[1024,128]{1,0:T(8,128)(2,1)S(1)}, u32[]{:S(2)}, u32[]{:S(2)}) %collective-permute-start.1) | collective-permute-done | bytes 262176 | tf_op jit(solution)/shard_map/ppermute | solution.py:519
  56.3 0.7 copy-done.8
  57.0 0.2 select_reduce_fusion
  57.2 0.0 copy-start.10
  57.3 0.7 copy-done.10
  57.9 0.0 collective-permute-done.4.oth1
  58.0 0.9 copy-done.7
  58.9 0.9 copy-done.9
  59.9 0.9 copy-done.11
  60.8 7.5 %shard_map.181 = (bf16[1024,256]{1,0:T(8,128)(2,1)S(1)}, bf16[3072,128]{1,0:T(8,128)(2,1)S(1)}, bf16[3072,128]{1,0:T(8,128)(2,1)S(1)}) custom-call(s32[1]{0:T(128)} %bitcast.8.core, s32[1024]{0:T(1024)S(1)} %broadcast_subtract_fusion.starts, bf16[1024,384]{1,0:T(8,128)(2,1)S(1)} %bitcast.27, bf16[1024,128]{1,0:T(8,128)(2,1)S(1)} %copy-done.9, ...), custom_call_target="tpu_custom_call" | custom-call | tf_op jit(solution)/shard_map/pallas_call | solution.py:492
  68.4 0.8 copy-done.4
  69.2 0.9 copy-done.19
  70.1 0.5 collective-permute-start.10
  70.5 0.7 collective-permute-start
  71.2 0.1 slice.12
  71.3 1.3 collective-permute-done.10.come_ref
  72.7 1.0 copy-done.5
  73.7 0.2 shard_map.184
  73.9 1.0 copy-done.1
  75.0 8.6 %all-to-all-start.2 = ((bf16[32,32,640]{2,1,0:T(8,128)(2,1)}), bf16[32,32,640]{2,1,0:T(8,128)(2,1)S(1)}, u32[]{:S(2)}, u32[]{:S(2)}) async-start(bf16[32,32,640]{2,1,0:T(8,128)(2,1)} %bitcast.25), calls=%async_computation.2 | async-start | bytes 2621440 | tf_op jit(solution)/shard_map/all_to_all | solution.py:523
  83.6 0.2 select_reduce_fusion.2
  83.8 0.1 pad.5.clone
  83.9 0.1 add_add_fusion.info
  83.9 0.1 constant_dynamic-slice_fusion
  84.0 2.8 %shard_map.182 = (f32[8,128,256]{2,1,0:T(8,128)S(1)}, f32[8,128,256]{2,1,0:T(8,128)S(1)}, f32[16,256]{1,0:T(8,128)S(1)}, bf16[144,256]{1,0:T(8,128)(2,1)S(1)}, bf16[144,256]{1,0:T(8,128)(2,1)S(1)}) custom-call(s32[4,8]{1,0:T(4,128)S(1)} %add_add_fusion.info, f32[4]{0:T(128)S(1)} %get-tuple-element.67.rates, bf16[1024,896]{1,0:T(8,128)(2,1)S(1)} %bitcast.23), custom_call_target="tpu_custom_call" | custom-call | tf_op jit(solution)/shard_map/pallas_call | solution.py:270
  86.8 10.5 %collective-permute-start.7 = (bf16[144,256]{1,0:T(8,128)(2,1)S(1)}, bf16[144,256]{1,0:T(8,128)(2,1)S(1)}, u32[]{:S(2)}, u32[]{:S(2)}) collective-permute-start(bf16[144,256]{1,0:T(8,128)(2,1)S(1)} %get-tuple-element.46), channel_id=1, source_target_pairs={{0,64},{32,96},{64,128},{96,160},{128,192},{160,224},{1,65},{33,97... | collective-permute-start | bytes 221192 | tf_op jit(solution)/shard_map/ppermute | solution.py:519
  97.4 1.9 %collective-permute-start.6 = (bf16[144,256]{1,0:T(8,128)(2,1)S(1)}, bf16[144,256]{1,0:T(8,128)(2,1)S(1)}, u32[]{:S(2)}, u32[]{:S(2)}) collective-permute-start(bf16[144,256]{1,0:T(8,128)(2,1)S(1)} %get-tuple-element.46), channel_id=1, source_target_pairs={{0,32},{32,64},{64,96},{96,128},{128,160},{160,192},{192,224},{1,3... | collective-permute-start | bytes 221192 | tf_op jit(solution)/shard_map/ppermute | solution.py:519
  99.3 3.1 %collective-permute-start.9 = (bf16[144,256]{1,0:T(8,128)(2,1)S(1)}, bf16[144,256]{1,0:T(8,128)(2,1)S(1)}, u32[]{:S(2)}, u32[]{:S(2)}) collective-permute-start(bf16[144,256]{1,0:T(8,128)(2,1)S(1)} %get-tuple-element.47), channel_id=1, source_target_pairs={{64,0},{96,32},{128,64},{160,96},{192,128},{224,160},{65,1},{97,33... | collective-permute-start | bytes 221192 | tf_op jit(solution)/shard_map/ppermute | solution.py:519
  102.4 2.1 %collective-permute-start.8 = (bf16[144,256]{1,0:T(8,128)(2,1)S(1)}, bf16[144,256]{1,0:T(8,128)(2,1)S(1)}, u32[]{:S(2)}, u32[]{:S(2)}) collective-permute-start(bf16[144,256]{1,0:T(8,128)(2,1)S(1)} %get-tuple-element.47), channel_id=1, source_target_pairs={{32,0},{64,32},{96,64},{128,96},{160,128},{192,160},{224,192},{33,... | collective-permute-start | bytes 221192 | tf_op jit(solution)/shard_map/ppermute | solution.py:519
  104.5 0.1 bitcast_subtract_fusion.ends_ref
  104.6 4.4 %collective-permute-done.9.b2 = bf16[144,256]{1,0:T(8,128)(2,1)S(1)} collective-permute-done((bf16[144,256]{1,0:T(8,128)(2,1)S(1)}, bf16[144,256]{1,0:T(8,128)(2,1)S(1)}, u32[]{:S(2)}, u32[]{:S(2)}) %collective-permute-start.9) | collective-permute-done | bytes 73760 | tf_op jit(solution)/shard_map/ppermute | solution.py:519
  109.0 0.9 collective-permute-done.8.b1
  109.9 9.6 %shard_map.183 = bf16[1024,768]{1,0:T(8,128)(2,1)} custom-call(s32[4,8]{1,0:T(4,128)S(1)} %add_add_fusion.info, f32[4]{0:T(128)S(1)} %get-tuple-element.67.rates, f32[4]{0:T(128)S(1)} %get-tuple-element.66.skips, bf16[1024,896]{1,0:T(8,128)(2,1)S(1)} %bitcast.24, s32[8,128]{1,0:T(8,128)S(1)} %bitcast_subtract_fusion.ends_ref, ...), custom_call_target="tpu_custom_call" | custom-call | tf_op jit(solution)/shard_map/pallas_call | solution.py:365
  119.4 7.2 %all-to-all-start.3 = ((bf16[32,32,768]{2,1,0:T(8,128)(2,1)}), bf16[32,32,768]{2,1,0:T(8,128)(2,1)S(1)}, u32[]{:S(2)}, u32[]{:S(2)}) async-start(bf16[32,32,768]{2,1,0:T(8,128)(2,1)} %bitcast.13), calls=%async_computation.3 | async-start | bytes 3145728 | tf_op jit(solution)/shard_map/all_to_all | solution.py:523
  126.7 1.5 shard_map.186
  128.2 1.9 %collective-permute-start.11 = (bf16[32,2048]{1,0:T(8,128)(2,1)S(1)}, bf16[32,2048]{1,0:T(8,128)(2,1)S(1)}, u32[]{:S(2)}, u32[]{:S(2)}) collective-permute-start(bf16[32,2048]{1,0:T(8,128)(2,1)S(1)} %get-tuple-element.60), channel_id=1, source_target_pairs={{32,0},{64,32},{96,64},{128,96},{160,128},{192,160},{224,192},{33,... | collective-permute-start | bytes 393224 | tf_op jit(solution)/shard_map/ppermute | solution.py:519
  130.1 1.9 %collective-permute-start.12 = (bf16[32,2048]{1,0:T(8,128)(2,1)S(1)}, bf16[32,2048]{1,0:T(8,128)(2,1)S(1)}, u32[]{:S(2)}, u32[]{:S(2)}) collective-permute-start(bf16[32,2048]{1,0:T(8,128)(2,1)S(1)} %get-tuple-element.61), channel_id=1, source_target_pairs={{64,0},{96,32},{128,64},{160,96},{192,128},{224,160},{65,1},{97,33... | collective-permute-start | bytes 393224 | tf_op jit(solution)/shard_map/ppermute | solution.py:519
  132.0 4.5 %collective-permute-done.11.one_ref = bf16[32,2048]{1,0:T(8,128)(2,1)S(1)} collective-permute-done((bf16[32,2048]{1,0:T(8,128)(2,1)S(1)}, bf16[32,2048]{1,0:T(8,128)(2,1)S(1)}, u32[]{:S(2)}, u32[]{:S(2)}) %collective-permute-start.11) | collective-permute-done | bytes 131104 | tf_op jit(solution)/shard_map/ppermute | solution.py:519
  136.5 7.1 %collective-permute-done.12.two_ref = bf16[32,2048]{1,0:T(8,128)(2,1)S(1)} collective-permute-done((bf16[32,2048]{1,0:T(8,128)(2,1)S(1)}, bf16[32,2048]{1,0:T(8,128)(2,1)S(1)}, u32[]{:S(2)}, u32[]{:S(2)}) %collective-permute-start.12) | collective-permute-done | bytes 131104 | tf_op jit(solution)/shard_map/ppermute | solution.py:519
  143.7 0.7 shard_map.187
  144.4 4.8 %all-to-all-done.3.in_ref = bf16[32,32,768]{2,1,0:T(8,128)(2,1)S(1)} async-done(((bf16[32,32,768]{2,1,0:T(8,128)(2,1)}), bf16[32,32,768]{2,1,0:T(8,128)(2,1)S(1)}, u32[]{:S(2)}, u32[]{:S(2)}) %all-to-all-start.3) | async-done | bytes 1572896 | tf_op jit(solution)/shard_map/all_to_all | solution.py:523
  149.2 1.6 %shard_map.185 = (bf16[32,8192]{1,0:T(8,128)(2,1)}, bf16[32,8192]{1,0:T(8,128)(2,1)}, bf16[32,1024]{1,0:T(8,128)(2,1)}, bf16[32,1024]{1,0:T(8,128)(2,1)}) custom-call(bf16[32,32,768]{2,1,0:T(8,128)(2,1)S(1)} %all-to-all-done.3.in_ref), custom_call_target="tpu_custom_call" | custom-call | tf_op jit(solution)/shard_map/pallas_call | solution.py:109
  (46 shorter events, 0.1 us)
Async XLA Ops:
  0.6 12.6 %copy-start.2 = (bf16[32,8192]{1,0:T(8,128)(2,1)S(1)}, bf16[32,8192]{1,0:T(8,128)(2,1)}, u32[]{:S(2)}) copy-start(bf16[32,8192]{1,0:T(8,128)(2,1)} %x_ref) | copy-start | bytes 1572868
  0.6 1.0 copy-start.12
  1.7 0.9 copy-start.13
  2.6 0.8 copy-start.14
  3.4 0.8 copy-start.15
  4.3 8.9 %copy-start.16 = (bf16[32,1024]{1,0:T(8,128)(2,1)S(1)}, bf16[32,1024]{1,0:T(8,128)(2,1)}, u32[]{:S(2)}) copy-start(bf16[32,1024]{1,0:T(8,128)(2,1)} %b_ref.1) | copy-start | bytes 196612
  4.3 8.9 %copy-start.17 = (bf16[32,1024]{1,0:T(8,128)(2,1)S(1)}, bf16[32,1024]{1,0:T(8,128)(2,1)}, u32[]{:S(2)}) copy-start(bf16[32,1024]{1,0:T(8,128)(2,1)} %c_ref.1) | copy-start | bytes 196612
  4.3 9.0 %copy-start.18 = (bf16[32,128]{1,0:T(8,128)(2,1)S(1)}, bf16[32,128]{1,0:T(8,128)(2,1)}, u32[]{:S(2)}) copy-start(bf16[32,128]{1,0:T(8,128)(2,1)} %dt_ref.1) | copy-start | bytes 24580
  5.9 21.7 %all-to-all-start = ((bf16[32,32,384]{2,1,0:T(8,128)(2,1)}), bf16[32,32,384]{2,1,0:T(8,128)(2,1)S(1)}, u32[]{:S(2)}, u32[]{:S(2)}) async-start(bf16[32,32,384]{2,1,0:T(8,128)(2,1)} %shard_map.179), calls=%async_computation | async-start | bytes 1572864 | tf_op jit(solution)/shard_map/all_to_all | solution.py:523
  13.2 1.0 copy-start.3
  14.7 1.3 copy-start
  15.9 25.8 %copy-start.20 = (s32[64]{0:T(128)S(1)}, s32[64]{0:T(128)}, u32[]{:S(2)}) copy-start(s32[64]{0:T(128)} %param.21) | copy-start | bytes 772
  27.6 42.4 %all-to-all-start.1 = ((bf16[32,32,896]{2,1,0:T(8,128)(2,1)}), bf16[32,32,896]{2,1,0:T(8,128)(2,1)S(1)}, u32[]{:S(2)}, u32[]{:S(2)}) async-start(bf16[32,32,896]{2,1,0:T(8,128)(2,1)} %copy-done), calls=%async_computation.1 | async-start | bytes 3670016 | tf_op jit(solution)/shard_map/all_to_all | solution.py:523
  31.7 38.9 %copy-start.21 = (f32[32]{0:T(128)S(1)}, f32[32]{0:T(128)}, u32[]{:S(2)}) copy-start(f32[32]{0:T(128)} %param.17) | copy-start | bytes 388
  31.7 38.8 %copy-start.22 = (f32[32]{0:T(128)S(1)}, f32[32]{0:T(128)}, u32[]{:S(2)}) copy-start(f32[32]{0:T(128)} %param.16) | copy-start | bytes 388
  32.4 18.9 %collective-permute-start.2 = (bf16[1024,128]{1,0:T(8,128)(2,1)}, bf16[1024,128]{1,0:T(8,128)(2,1)S(1)}, u32[]{:S(2)}, u32[]{:S(2)}) collective-permute-start(bf16[1024,128]{1,0:T(8,128)(2,1)} %slice.16), channel_id=1, source_target_pairs={{0,64},{32,96},{64,128},{96,160},{128,192},{160,224},{1,65},{33,97... | collective-permute-start | bytes 786440 | tf_op jit(solution)/shard_map/ppermute | solution.py:519
  38.8 17.5 %collective-permute-start.1 = (bf16[1024,128]{1,0:T(8,128)(2,1)}, bf16[1024,128]{1,0:T(8,128)(2,1)S(1)}, u32[]{:S(2)}, u32[]{:S(2)}) collective-permute-start(bf16[1024,128]{1,0:T(8,128)(2,1)} %slice.16), channel_id=1, source_target_pairs={{0,32},{32,64},{64,96},{96,128},{128,160},{160,192},{192,224},{1,3... | collective-permute-start | bytes 786440 | tf_op jit(solution)/shard_map/ppermute | solution.py:519
  42.1 15.1 %collective-permute-start.3 = (bf16[1024,128]{1,0:T(8,128)(2,1)}, bf16[1024,128]{1,0:T(8,128)(2,1)S(1)}, u32[]{:S(2)}, u32[]{:S(2)}) collective-permute-start(bf16[1024,128]{1,0:T(8,128)(2,1)} %slice.16), channel_id=1, source_target_pairs={{0,4},{4,0},{1,5},{5,1},{2,6},{6,2},{3,7},{7,3},{8,12},{12,8},{9,1... | collective-permute-start | bytes 786440 | tf_op jit(solution)/shard_map/ppermute | solution.py:527
  51.4 6.6 %collective-permute-start.5 = (bf16[1024,128]{1,0:T(8,128)(2,1)S(1)}, bf16[1024,128]{1,0:T(8,128)(2,1)}, u32[]{:S(2)}, u32[]{:S(2)}) collective-permute-start(bf16[1024,128]{1,0:T(8,128)(2,1)S(1)} %collective-permute-done.2.own2), channel_id=1, source_target_pairs={{0,4},{4,0},{1,5},{5,1},{2,6},{6,2},{3,7},{7,3},{8,12},{12,8},{9,1... | collective-permute-start | bytes 786440 | tf_op jit(solution)/shard_map/ppermute | solution.py:527
  51.4 0.7 copy-start.6
  56.3 1.7 %collective-permute-start.4 = (bf16[1024,128]{1,0:T(8,128)(2,1)S(1)}, bf16[1024,128]{1,0:T(8,128)(2,1)}, u32[]{:S(2)}, u32[]{:S(2)}) collective-permute-start(bf16[1024,128]{1,0:T(8,128)(2,1)S(1)} %collective-permute-done.1.own1), channel_id=1, source_target_pairs={{0,4},{4,0},{1,5},{5,1},{2,6},{6,2},{3,7},{7,3},{8,12},{12,8},{9,1... | collective-permute-start | bytes 786440 | tf_op jit(solution)/shard_map/ppermute | solution.py:527
  56.3 0.7 copy-start.8
  57.2 0.7 copy-start.10
  58.0 1.0 copy-start.7
  58.9 0.9 copy-start.9
  59.9 0.9 copy-start.11
  68.4 0.8 copy-start.4
  69.2 0.9 copy-start.19
  70.1 2.6 %collective-permute-start.10 = (bf16[3072,128]{1,0:T(8,128)(2,1)}, bf16[3072,128]{1,0:T(8,128)(2,1)S(1)}, u32[]{:S(2)}, u32[]{:S(2)}) collective-permute-start(bf16[3072,128]{1,0:T(8,128)(2,1)} %copy-done.19), channel_id=1, source_target_pairs={{0,4},{4,0},{1,5},{5,1},{2,6},{6,2},{3,7},{7,3},{8,12},{12,8},{9,1... | collective-permute-start | bytes 2359304 | tf_op jit(solution)/shard_map/ppermute | solution.py:527
  70.5 13.4 %collective-permute-start = (f32[2,32]{1,0:T(2,128)S(1)}, f32[2,32]{1,0:T(2,128)S(1)}, u32[]{:S(2)}, u32[]{:S(2)}) collective-permute-start(f32[2,32]{1,0:T(2,128)S(1)} %pad_maximum_fusion), channel_id=1, source_target_pairs={{0,0},{1,8},{2,16},{3,24},{8,1},{9,9},{10,17},{11,25},{16,2},{17,1... | collective-permute-start | bytes 776 | tf_op jit(solution)/shard_map/ppermute | solution.py:538
  72.6 1.0 copy-start.5
  73.9 1.1 copy-start.1
  75.0 44.4 %all-to-all-start.2 = ((bf16[32,32,640]{2,1,0:T(8,128)(2,1)}), bf16[32,32,640]{2,1,0:T(8,128)(2,1)S(1)}, u32[]{:S(2)}, u32[]{:S(2)}) async-start(bf16[32,32,640]{2,1,0:T(8,128)(2,1)} %bitcast.25), calls=%async_computation.2 | async-start | bytes 2621440 | tf_op jit(solution)/shard_map/all_to_all | solution.py:523
  86.8 17.8 %collective-permute-start.7 = (bf16[144,256]{1,0:T(8,128)(2,1)S(1)}, bf16[144,256]{1,0:T(8,128)(2,1)S(1)}, u32[]{:S(2)}, u32[]{:S(2)}) collective-permute-start(bf16[144,256]{1,0:T(8,128)(2,1)S(1)} %get-tuple-element.46), channel_id=1, source_target_pairs={{0,64},{32,96},{64,128},{96,160},{128,192},{160,224},{1,65},{33,97... | collective-permute-start | bytes 221192 | tf_op jit(solution)/shard_map/ppermute | solution.py:519
  97.4 7.2 %collective-permute-start.6 = (bf16[144,256]{1,0:T(8,128)(2,1)S(1)}, bf16[144,256]{1,0:T(8,128)(2,1)S(1)}, u32[]{:S(2)}, u32[]{:S(2)}) collective-permute-start(bf16[144,256]{1,0:T(8,128)(2,1)S(1)} %get-tuple-element.46), channel_id=1, source_target_pairs={{0,32},{32,64},{64,96},{96,128},{128,160},{160,192},{192,224},{1,3... | collective-permute-start | bytes 221192 | tf_op jit(solution)/shard_map/ppermute | solution.py:519
  99.3 9.7 %collective-permute-start.9 = (bf16[144,256]{1,0:T(8,128)(2,1)S(1)}, bf16[144,256]{1,0:T(8,128)(2,1)S(1)}, u32[]{:S(2)}, u32[]{:S(2)}) collective-permute-start(bf16[144,256]{1,0:T(8,128)(2,1)S(1)} %get-tuple-element.47), channel_id=1, source_target_pairs={{64,0},{96,32},{128,64},{160,96},{192,128},{224,160},{65,1},{97,33... | collective-permute-start | bytes 221192 | tf_op jit(solution)/shard_map/ppermute | solution.py:519
  102.4 7.4 %collective-permute-start.8 = (bf16[144,256]{1,0:T(8,128)(2,1)S(1)}, bf16[144,256]{1,0:T(8,128)(2,1)S(1)}, u32[]{:S(2)}, u32[]{:S(2)}) collective-permute-start(bf16[144,256]{1,0:T(8,128)(2,1)S(1)} %get-tuple-element.47), channel_id=1, source_target_pairs={{32,0},{64,32},{96,64},{128,96},{160,128},{192,160},{224,192},{33,... | collective-permute-start | bytes 221192 | tf_op jit(solution)/shard_map/ppermute | solution.py:519
  119.4 29.7 %all-to-all-start.3 = ((bf16[32,32,768]{2,1,0:T(8,128)(2,1)}), bf16[32,32,768]{2,1,0:T(8,128)(2,1)S(1)}, u32[]{:S(2)}, u32[]{:S(2)}) async-start(bf16[32,32,768]{2,1,0:T(8,128)(2,1)} %bitcast.13), calls=%async_computation.3 | async-start | bytes 3145728 | tf_op jit(solution)/shard_map/all_to_all | solution.py:523
  128.2 8.4 %collective-permute-start.11 = (bf16[32,2048]{1,0:T(8,128)(2,1)S(1)}, bf16[32,2048]{1,0:T(8,128)(2,1)S(1)}, u32[]{:S(2)}, u32[]{:S(2)}) collective-permute-start(bf16[32,2048]{1,0:T(8,128)(2,1)S(1)} %get-tuple-element.60), channel_id=1, source_target_pairs={{32,0},{64,32},{96,64},{128,96},{160,128},{192,160},{224,192},{33,... | collective-permute-start | bytes 393224 | tf_op jit(solution)/shard_map/ppermute | solution.py:519
  130.1 13.6 %collective-permute-start.12 = (bf16[32,2048]{1,0:T(8,128)(2,1)S(1)}, bf16[32,2048]{1,0:T(8,128)(2,1)S(1)}, u32[]{:S(2)}, u32[]{:S(2)}) collective-permute-start(bf16[32,2048]{1,0:T(8,128)(2,1)S(1)} %get-tuple-element.61), channel_id=1, source_target_pairs={{64,0},{96,32},{128,64},{160,96},{192,128},{224,160},{65,1},{97,33... | collective-permute-start | bytes 393224 | tf_op jit(solution)/shard_map/ppermute | solution.py:519

commit v2 on v1

--- a/solution.py
+++ b/solution.py
@@ -20,10 +20,9 @@
 SCALE = 128 ** (-0.5)
 TQ = 512
 TK = 512
-PAD = 0
 UNROLL = 2
+ATT = 5
 NEG = -1e30
-VMEM = 36 * 1024 * 1024
 NN = (((1,), (0,)), ((), ()))
 NT = (((1,), (1,)), ((), ()))
 TN = (((0,), (0,)), ((), ()))
@@ -33,8 +32,20 @@
     return lax.dot_general(a, b, dims, preferred_element_type=F32)
 
 
-def params():
-    return pltpu.CompilerParams(vmem_limit_bytes=VMEM)
+def params(mib=8):
+    return pltpu.CompilerParams(vmem_limit_bytes=mib * 1024 * 1024)
+
+
+def in_hbm(*arrays):
+    return [pltpu.with_memory_space_constraint(a, pltpu.HBM) for a in arrays]
+
+
+def in_vmem(*arrays):
+    return [pltpu.with_memory_space_constraint(a, pltpu.VMEM) for a in arrays]
+
+
+def cost(micros):
+    return pl.CostEstimate(flops=int(micros * 10**9), bytes_accessed=10**6, transcendentals=0)
 
 
 def smem():
@@ -77,9 +88,9 @@
         grid=(4,),
         in_specs=[wide(2048), wide(2048), wide(256), wide(256), pl.BlockSpec((ROWS, 128), lambda y: (0, 0))],
         out_specs=pl.BlockSpec((8, ROWS, 896), lambda y: (y, 0, 0)),
-        out_shape=jax.ShapeDtypeStruct((32, ROWS, 896), BF),
+        out_shape=pltpu.HBM((32, ROWS, 896), BF),
         compiler_params=params(),
-    )(xs, gy, bs, cs, dts)
+    )(*in_hbm(xs, gy, bs, cs, dts))
 
 
 def do_pack_attention(q, ga, keys, values):
@@ -88,9 +99,9 @@
         grid=(4,),
         in_specs=[wide(1024), wide(1024), wide(256), wide(256)],
         out_specs=pl.BlockSpec((8, ROWS, 384), lambda y: (y, 0, 0)),
-        out_shape=jax.ShapeDtypeStruct((32, ROWS, 384), BF),
+        out_shape=pltpu.HBM((32, ROWS, 384), BF),
         compiler_params=params(),
-    )(q, ga, keys, values)
+    )(*in_hbm(q, ga, keys, values))
 
 
 def unpack_mixer(in_ref, y_ref, gx_ref, gb_ref, gc_ref):
@@ -184,9 +195,9 @@
         pack_back,
         in_specs=[vmem()] * 3,
         out_specs=vmem(),
-        out_shape=jax.ShapeDtypeStruct((SUPER, 640), BF),
+        out_shape=pltpu.HBM((SUPER, 640), BF),
         compiler_params=params(),
-    )(att, keep, come)
+    )(*in_hbm(att, keep), come)
 
 
 def lane_row(values, width):
@@ -225,7 +236,9 @@
     return steps, steps * weight, enter, end
 
 
-def state_kernel(info, rates, in_ref, inc_ref, out_ref, factor_ref, sf_ref, sb_ref):
+def state_kernel(
+    info, rates, in_ref, inc_ref, out_ref, factor_ref, sf_ref, sb_ref, low_ref, full_ref
+):
     first = info[3, 0] * HEADS
     tri = lower(BLOCK)
     chooser = pick(first, WIDTH)
@@ -242,6 +255,10 @@
         )
         scaled = (in_ref[rows, 0:256].astype(F32) * weighted).astype(BF)
         dcar = (in_ref[rows, 256:512].astype(F32) * enter).astype(BF)
+        low_ref[rows, 0:256] = scaled
+        low_ref[rows, 256:512] = dcar
+        full_ref[rows, 0:256] = weighted
+        full_ref[rows, 256:512] = enter
         carry = jnp.where(alive > 0, jnp.exp(end), 0.0)
         inc_ref[j] = state
         factor_ref[j : j + 1, :] = prefix
@@ -270,16 +287,19 @@
     return pl.pallas_call(
         state_kernel,
         in_specs=[smem(), smem(), vmem()],
-        out_specs=[vmem()] * 5,
+        out_specs=[vmem()] * 7,
         out_shape=[
-            jax.ShapeDtypeStruct((BLOCKS, STATE, CH), F32),
-            jax.ShapeDtypeStruct((BLOCKS, STATE, CH), F32),
-            jax.ShapeDtypeStruct((16, CH), F32),
+            pltpu.VMEM((BLOCKS, STATE, CH), F32),
+            pltpu.VMEM((BLOCKS, STATE, CH), F32),
+            pltpu.VMEM((16, CH), F32),
             jax.ShapeDtypeStruct((144, CH), BF),
             jax.ShapeDtypeStruct((144, CH), BF),
+            pltpu.VMEM((SUPER, 512), BF),
+            pltpu.VMEM((SUPER, 512), F32),
         ],
-        compiler_params=params(),
-    )(info, rates, got)
+        compiler_params=params(12),
+        cost_estimate=cost(3),
+    )(info, rates, *in_vmem(got))
 
 
 def joined(one_ref, two_ref):
@@ -287,9 +307,7 @@
     return one_ref[0:128, :].astype(F32) + decay * two_ref[0:128, :].astype(F32)
 
 
-def mixer_kernel(
-    info, rates, skips, in_ref, ends_ref, inc_ref, back_ref, factor_ref, f1, f2, b1, b2, out_ref
-):
+def inner_kernel(info, rates, skips, in_ref, ends_ref, out_ref):
     first = info[3, 0] * HEADS
     tri = lower(BLOCK)
     triu = upper(BLOCK)
@@ -298,10 +316,7 @@
     head_row = lax.broadcasted_iota(jnp.int32, (8, 128), 0)
     head_at = lax.broadcasted_iota(jnp.int32, (8, 128), 1) - first
     row_chooser = ((head_row == head_at) & (head_row < HEADS)).astype(F32).astype(BF)
-    rate_row = lane_row([rates[h] for h in range(HEADS)], WIDTH)
     skip_row = lane_row([skips[h] for h in range(HEADS)], WIDTH)
-    entering = joined(f1, f2)
-    leaving = joined(b1, b2)
     t_at = lax.broadcasted_iota(jnp.int32, (BLOCK, BLOCK), 0)
     s_at = lax.broadcasted_iota(jnp.int32, (BLOCK, BLOCK), 1)
     lane = lax.broadcasted_iota(jnp.int32, (BLOCK, CH), 1)
@@ -309,16 +324,12 @@
 
     def one(j, _):
         rows = pl.ds(pl.multiple_of(j * BLOCK, BLOCK), BLOCK)
-        tail, entry = info[0, j], info[1, j]
         dts = in_ref[rows, 768:896]
-        steps, weighted, enter, _ = channel_decay(dts, chooser, tri, rate_row, tail, entry)
+        steps = dot(dts, chooser)
         x = in_ref[rows, 0:256].astype(F32)
         gy_low = in_ref[rows, 256:512]
-        gy = gy_low.astype(F32)
         b = in_ref[rows, 512:640]
         c = in_ref[rows, 640:768]
-        state = (inc_ref[j] + factor_ref[pl.ds(j, 1), :] * entering).astype(BF)
-        pull = (back_ref[j] + factor_ref[pl.ds(8 + j, 1), :] * leaving).astype(BF)
         columns = dot(tri, dot(dts, column_chooser).astype(BF))
         lines = dot(dot(row_chooser, dts, NT).astype(BF), triu)
         ends = ends_ref[pl.ds(j, 1), :]
@@ -336,8 +347,7 @@
             drives.append(jnp.where(owns[h], driven, 0.0).astype(BF))
         mix = jnp.concatenate(mixes, axis=1)
         drive = jnp.concatenate(drives, axis=0)
-        y = dot(mix, drive) + dot(c, state) * enter + skip_row * x
-        out_ref[rows, 0:256] = y.astype(BF)
+        out_ref[rows, 0:256] = dot(mix, drive) + skip_row * x
         grad_mix = dot(gy_low, drive, NT)
         grad_scores = decays[0] * grad_mix[:, 0:128]
         for h in range(1, HEADS):
@@ -347,57 +357,93 @@
         grad_drive = jnp.where(owns[0], back[0:128], 0.0)
         for h in range(1, HEADS):
             grad_drive = jnp.where(owns[h], back[h * 128 : h * 128 + 128], grad_drive)
-        grad_scaled = dot(b, pull)
-        gx = grad_drive * steps + grad_scaled * weighted + skip_row * gy
+        out_ref[rows, 256:512] = grad_drive * steps + skip_row * gy_low.astype(F32)
+        out_ref[rows, 512:640] = dot(grad_low, c, TN)
+        out_ref[rows, 640:768] = dot(grad_low, b)
+        return 0
+
+    lax.fori_loop(0, BLOCKS, one, 0, unroll=UNROLL)
+
+
+def do_inner(info, rates, skips, got, ends):
+    return pl.pallas_call(
+        inner_kernel,
+        in_specs=[smem()] * 3 + [vmem()] * 2,
+        out_specs=vmem(),
+        out_shape=pltpu.VMEM((SUPER, 768), F32),
+        compiler_params=params(12),
+        cost_estimate=cost(8),
+    )(info, rates, skips, *in_vmem(got), ends)
+
+
+def outer_kernel(
+    in_ref, part_ref, low_ref, full_ref, inc_ref, back_ref, factor_ref, f1, f2, b1, b2, out_ref
+):
+    entering = joined(f1, f2)
+    leaving = joined(b1, b2)
+    for j in range(BLOCKS):
+        rows = slice(j * BLOCK, j * BLOCK + BLOCK)
+        b = in_ref[rows, 512:640]
+        c = in_ref[rows, 640:768]
+        state = (inc_ref[j] + factor_ref[j : j + 1, :] * entering).astype(BF)
+        pull = (back_ref[j] + factor_ref[8 + j : 9 + j, :] * leaving).astype(BF)
+        y = part_ref[rows, 0:256] + dot(c, state) * full_ref[rows, 256:512]
+        gx = part_ref[rows, 256:512] + dot(b, pull) * full_ref[rows, 0:256]
+        gb = part_ref[rows, 512:640] + dot(low_ref[rows, 0:256], pull, NT)
+        gc = part_ref[rows, 640:768] + dot(low_ref[rows, 256:512], state, NT)
+        out_ref[rows, 0:256] = y.astype(BF)
         out_ref[rows, 256:512] = gx.astype(BF)
-        scaled = (x * weighted).astype(BF)
-        dcar = (gy * enter).astype(BF)
-        gb = dot(grad_low, c, TN) + dot(scaled, pull, NT)
-        gc = dot(grad_low, b) + dot(dcar, state, NT)
         out_ref[rows, 512:640] = gb.astype(BF)
         out_ref[rows, 640:768] = gc.astype(BF)
-        return 0
-
-    lax.fori_loop(0, BLOCKS, one, 0, unroll=UNROLL)
-
-
-def do_mixer(info, rates, skips, got, ends, inc, back, factor, f1, f2, b1, b2):
-    return pl.pallas_call(
-        mixer_kernel,
-        in_specs=[smem()] * 3 + [vmem()] * 9,
+
+
+def do_outer(*operands):
+    return pl.pallas_call(
+        outer_kernel,
+        in_specs=[vmem()] * 11,
         out_specs=vmem(),
-        out_shape=jax.ShapeDtypeStruct((SUPER, 768), BF),
-        compiler_params=params(),
-    )(info, rates, skips, got, ends, inc, back, factor, f1, f2, b1, b2)
+        out_shape=pltpu.HBM((SUPER, 768), BF),
+        compiler_params=params(16),
+        cost_estimate=cost(2),
+    )(*in_vmem(*operands))
 
 
 def attention_kernel(
-    core, starts, in_ref, own1, own2, oth0, oth1, oth2, start_ref, out_ref, keep_ref, send_ref,
-    k_ref, v_ref, kt_ref, vt_ref, near_ref, far_ref, peak_ref, gk_ref, gv_ref
+    core, starts, in_ref, own0, own1, own2, oth0, oth1, oth2, start_ref, out_ref, keep_ref, send_ref,
+    k_ref, v_ref, kt_ref, vt_ref, near_ref, far_ref, peak_ref, gk_ref, gv_ref, sems
 ):
     count = SUPER // TQ
     lowest = starts[0] - TK + 1
+    places_of = [slice(n * SUPER, n * SUPER + SUPER) for n in range(3)]
+    owns = (own2, own1, own0)
+    others = (oth2, oth1, oth0)
+
+    def moves(n, first):
+        mine, theirs = (owns[n], others[n]) if first else (others[n], owns[n])
+        return (
+            pltpu.make_async_copy(mine, k_ref.at[places_of[n], :], sems.at[2 * n]),
+            pltpu.make_async_copy(theirs, v_ref.at[places_of[n], :], sems.at[2 * n + 1]),
+        )
+
+    def on_core(n, first, act):
+        @pl.when((lowest < (n + 1) * SUPER) & ((core[0] == 0) == first))
+        def _():
+            for move in moves(n, first):
+                act(move)
+
+    for n in (2, 1, 0):
+        on_core(n, True, lambda move: move.start())
+        on_core(n, False, lambda move: move.start())
     gk_ref[...] = jnp.zeros_like(gk_ref)
     gv_ref[...] = jnp.zeros_like(gv_ref)
-    for n in range(3):
-        rows = slice(PAD + n * SUPER, PAD + n * SUPER + SUPER)
-        own = (own2, own1, in_ref.at[:, 256:384])[n]
-        other = (oth2, oth1, oth0)[n]
-
-        @pl.when((lowest < (n + 1) * SUPER) & (core[0] == 0))
-        def _():
-            k_ref[rows, :] = own[...]
-            v_ref[rows, :] = other[...]
-
-        @pl.when((lowest < (n + 1) * SUPER) & (core[0] != 0))
-        def _():
-            k_ref[rows, :] = other[...]
-            v_ref[rows, :] = own[...]
+    for n in (2, 1, 0):
+        on_core(n, True, lambda move: move.wait())
+        on_core(n, False, lambda move: move.wait())
 
         @pl.when(lowest < (n + 1) * SUPER)
         def _():
-            kt_ref[:, rows] = k_ref[rows, :].T
-            vt_ref[:, rows] = v_ref[rows, :].T
+            kt_ref[:, places_of[n]] = k_ref[places_of[n], :].T
+            vt_ref[:, places_of[n]] = v_ref[places_of[n], :].T
 
     def tile_sum(p):
         return jnp.sum(p.reshape(p.shape[0] // 8, 8, TQ), axis=0)
@@ -407,7 +453,7 @@
     far_at = lax.broadcasted_iota(jnp.int32, (TK, TQ), 0)
     q_rows = [slice(i * TQ, i * TQ + TQ) for i in range(count)]
     diag = [2 * SUPER + i * TQ for i in range(count)]
-    near = [slice(PAD + diag[i], PAD + diag[i] + TQ) for i in range(count)]
+    near = [slice(diag[i], diag[i] + TQ) for i in range(count)]
     begins = [start_ref[i : i + 1, :] for i in range(count)]
     many = [(jnp.maximum(diag[i] - starts[i * TQ], 0) + TK - 1) // TK for i in range(count)]
 
@@ -428,7 +474,7 @@
         def forward(t, carry):
             peak, total, att = carry
             base = diag[i] - TK * (t + 1)
-            rows = pl.ds(pl.multiple_of(PAD + base, TQ), TK)
+            rows = pl.ds(pl.multiple_of(base, TQ), TK)
             s = dot(k_ref[rows, :], q, NT)
             s = jnp.where(far_at >= begins[i] - base, s, NEG)
             top = jnp.maximum(peak, jnp.max(s, axis=0, keepdims=True))
@@ -462,7 +508,7 @@
         ga = in_ref[q_rows[i], 128:256]
 
         def backward(t, gq):
-            rows = pl.ds(pl.multiple_of(PAD + diag[i] - TK * (t + 1), TQ), TK)
+            rows = pl.ds(pl.multiple_of(diag[i] - TK * (t + 1), TQ), TK)
             factor = jnp.exp((peak_ref[i, pl.ds(t, 1), :] - peak) * SCALE) * inverse
             probs = far_ref[i, t] * factor
             ds = (probs * (dot(v_ref[rows, :], ga, NT) - delta)).astype(BF)
@@ -474,8 +520,8 @@
         out_ref[q_rows[i], 128:256] = (gq * SCALE).astype(BF).T
 
     def store(k_out, v_out):
-        k_out[...] = (gk_ref[PAD:, :] * SCALE).astype(BF)
-        v_out[...] = gv_ref[PAD:, :].astype(BF)
+        k_out[...] = (gk_ref[...] * SCALE).astype(BF)
+        v_out[...] = gv_ref[...].astype(BF)
 
     @pl.when(core[0] == 0)
     def _():
@@ -486,17 +532,17 @@
         store(send_ref, keep_ref)
 
 
-def do_attention(core, starts, got, own1, own2, oth0, oth1, oth2):
-    span = PAD + 3 * SUPER
+def do_attention(core, starts, *moved):
+    span = 3 * SUPER
     count = SUPER // TQ
     return pl.pallas_call(
         attention_kernel,
-        in_specs=[smem(), smem()] + [vmem()] * 7,
+        in_specs=[smem()] * 2 + [vmem()] + [pl.BlockSpec(memory_space=pl.ANY)] * 6 + [vmem()],
         out_specs=[vmem()] * 3,
         out_shape=[
-            jax.ShapeDtypeStruct((SUPER, 256), BF),
-            jax.ShapeDtypeStruct((3 * SUPER, 128), BF),
-            jax.ShapeDtypeStruct((3 * SUPER, 128), BF),
+            pltpu.HBM((SUPER, 256), BF),
+            pltpu.HBM((3 * SUPER, 128), BF),
+            pltpu.HBM((3 * SUPER, 128), BF),
         ],
         scratch_shapes=[
             pltpu.VMEM((span, 128), BF),
@@ -508,9 +554,11 @@
             pltpu.VMEM((count, 8, TQ), F32),
             pltpu.VMEM((span, 128), F32),
             pltpu.VMEM((span, 128), F32),
+            pltpu.SemaphoreType.DMA((6,)),
         ],
-        compiler_params=params(),
-    )(core, starts, got, own1, own2, oth0, oth1, oth2, starts.reshape(SUPER // TQ, TQ))
+        compiler_params=params(28),
+        cost_estimate=cost(ATT),
+    )(core, starts, *moved, starts.reshape(SUPER // TQ, TQ))
 
 
 def shifted(block, distance):
@@ -534,13 +582,13 @@
 
     packed_a = do_pack_attention(queries, grad_attn, keys, values)
     packed_a, xs, rates = lax.optimization_barrier((packed_a, xs, rates))
+    packed_m = do_pack_mixer(xs, grad_y, bs, cs, dts)
     side = lax.axis_size("tp")
     both = lax.ppermute(
         jnp.stack([rates, skips]),
         ("y", "tp"),
         [(a * side + b, b * side + a) for a in range(side) for b in range(side)],
     )
-    packed_m = do_pack_mixer(xs, grad_y, bs, cs, dts)
     mine = lax.dynamic_slice_in_dim(both, inside * HEADS, HEADS, 1)
     my_rates, my_skips = mine[0], mine[1]
 
@@ -568,28 +616,30 @@
     )
     local_stops = (stops.reshape(BLOCKS, BLOCK) - block_at[:, None]).astype(jnp.int32)
 
-    got_a = exchange(packed_a)
-    packed_m, got_a = lax.optimization_barrier((packed_m, got_a))
+    got_a, packed_m = lax.optimization_barrier((exchange(packed_a), packed_m))
     got_a = got_a.reshape(SUPER, 384)
     own0 = got_a[:, 256:384]
     own1, own2 = shifted(own0, 1), shifted(own0, 2)
+    oth0 = swapped(own0)
+    packed_m, oth0, my_rates, my_skips = lax.optimization_barrier(
+        (packed_m, oth0, my_rates, my_skips)
+    )
     got = exchange(packed_m)
     att, keep, send = do_attention(
         jnp.full((1,), core, jnp.int32),
         (starts - (base - 2 * SUPER)).astype(jnp.int32),
-        got_a, own1, own2, swapped(own0), swapped(own1), swapped(own2),
+        got_a, own0, own1, own2, oth0, swapped(own1), swapped(own2),
     )
-    send, got = lax.optimization_barrier((send, got))
+    packed_b = do_pack_back(att, keep, swapped(send))
+    packed_b, got = lax.optimization_barrier((packed_b, got))
+    out_a = exchange(packed_b.reshape(32, ROWS, 640))
     got = got.reshape(SUPER, 896)
-    packed_b = do_pack_back(att, keep, swapped(send))
-    out_a = exchange(packed_b.reshape(32, ROWS, 640))
-
-    inc, back, factor, send_f, send_b = do_state(info, my_rates, got)
+    inc, back, factor, send_f, send_b, low, full = do_state(info, my_rates, got)
+    got, low = lax.optimization_barrier((got, low))
     f1, f2 = shifted(send_f, 1), shifted(send_f, 2)
     b1, b2 = shifted(send_b, -1), shifted(send_b, -2)
-    mixed = do_mixer(
-        info, my_rates, my_skips, got, local_stops, inc, back, factor, f1, f2, b1, b2
-    )
+    inner = do_inner(info, my_rates, my_skips, got, local_stops)
+    mixed = do_outer(got, inner, low, full, inc, back, factor, f1, f2, b1, b2)
     mixed, out_a = lax.optimization_barrier((mixed, out_a))
     out_m = exchange(mixed.reshape(32, ROWS, 768))
     att, gq, p2, p1, p0 = do_unpack_attention(out_a)

time: 154 us -> 135 us (0.88); the launches traced: 151 us -> 135 us
  local copies, waits for them, and re-layouts: 15.7 us -> 0.38 us
  Pallas kernels: 25.8 us -> 34.7 us
  waiting for transfers between devices: 48.3 us -> 40.2 us
    unnamed x46 -> x6, local copies, waits for them, and re-layouts: 14.7 us -> 0.01 us
    ppermute x8, waiting for transfers between devices: 30.4 us -> 22.7 us  [shifted(): return lax.ppermute(block, 'z', route)]
    all_to_all x4, starting transfers between devices: 27.2 us -> 22.8 us  [exchange(): return lax.all_to_all(block, GROUP, split_axis=0, concat_axis=0, tiled=True)]
    pallas_call x1, Pallas kernels: 0.38 us -> 3.64 us  [do_pack_mixer(): pl.pallas_call(pack_mixer, grid=(4,), in_specs=[wide(2048), wide(2048), w...]
    ppermute x8, starting transfers between devices: 30.8 us -> 33.9 us  [shifted(): return lax.ppermute(block, 'z', route)]
    all_to_all x4, waiting for transfers between devices: 16.5 us -> 13.7 us  [exchange(): return lax.all_to_all(block, GROUP, split_axis=0, concat_axis=0, tiled=True)]
    ppermute x4, waiting for transfers between devices: 1.39 us -> 3.75 us  [swapped(): return lax.ppermute(block, 'core', [(0, 1), (1, 0)])]
    pallas_call x1, Pallas kernels: 0.24 us -> 2.6 us  [do_pack_back(): pl.pallas_call(pack_back, in_specs=[vmem()] * 3, out_specs=vmem(), out_sh...]
  transfers between devices with their start and end apart: 17 -> 17, of which waited for: 9 -> 8; matrix products, arithmetic and copies ran while one was open for 1% -> 1% of each run, Pallas kernels for 15% -> 22%
where the time goes in v2:
time: 135 us
  starting transfers between devices  57.7 us (43%)
  waiting for transfers between devices  40.2 us (30%)
  Pallas kernels  34.7 us (26%)
    ppermute x8, starting transfers between devices, shifted(): return lax.ppermute(block, 'z', route)  33.9 us
    all_to_all x4, starting transfers between devices, exchange(): return lax.all_to_all(block, GROUP, split_axis=0, concat_axis=0, tiled=True)  22.8 us
    ppermute x8, waiting for transfers between devices, shifted(): return lax.ppermute(block, 'z', route)  22.7 us
    all_to_all x4, waiting for transfers between devices, exchange(): return lax.all_to_all(block, GROUP, split_axis=0, concat_axis=0, tiled=True)  13.7 us
    pallas_call x1, Pallas kernels, do_attention(): pl.pallas_call(attention_kernel, in_specs=[smem()] * 2 + [vmem()] + [pl.B...  9.05 us
    pallas_call x1, Pallas kernels, do_inner(): pl.pallas_call(inner_kernel, in_specs=[smem()] * 3 + [vmem()] * 2, out_sp...  7.64 us
    ppermute x4, waiting for transfers between devices, swapped(): return lax.ppermute(block, 'core', [(0, 1), (1, 0)])  3.75 us
    pallas_call x1, Pallas kernels, do_pack_mixer(): pl.pallas_call(pack_mixer, grid=(4,), in_specs=[wide(2048), wide(2048), w...  3.64 us
  transfers between devices with their start and end apart: 17, of which 8 were waited for; matrix products, arithmetic and copies ran while one was open for 1% of the time, Pallas kernels for 22%

profile of v2, /device:TPU:64, one launch (start us, length us, event | category | flops | bytes accessed | tf_op | source)
XLA Modules:
  0.0 134.7 jit_solution(12823214389656517433)
XLA Ops:
  0.6 0.0 copy-start.2
  0.6 0.0 copy-start.1
  0.7 0.0 copy-start
  0.7 3.2 %shard_map.179 = bf16[32,32,384]{2,1,0:T(8,128)(2,1)} custom-call(bf16[32,4096]{1,0:T(8,128)(2,1)} %q_ref.1, bf16[32,4096]{1,0:T(8,128)(2,1)} %ga_ref.1, bf16[32,1024]{1,0:T(8,128)(2,1)} %k_ref.1, bf16[32,1024]{1,0:T(8,128)(2,1)} %v_ref.1), custom_call_target="tpu_custom_call" | custom-call | tf_op jit(solution)/shard_map/pallas_call | solution.py:97
  3.9 7.3 %all-to-all-start = ((bf16[32,32,384]{2,1,0:T(8,128)(2,1)}), bf16[32,32,384]{2,1,0:T(8,128)(2,1)S(1)}, u32[]{:S(2)}, u32[]{:S(2)}) async-start(bf16[32,32,384]{2,1,0:T(8,128)(2,1)} %shard_map.179), calls=%async_computation | async-start | bytes 1572864 | tf_op jit(solution)/shard_map/all_to_all | solution.py:571
  11.2 0.0 copy-done.2
  11.2 0.0 copy-done.1
  11.3 0.7 collective-permute-start.3
  12.0 0.0 copy-done
  12.0 0.1 copy.22
  12.1 0.1 reduce-window.8
  12.2 0.1 reduce
  12.3 3.6 %shard_map.180 = bf16[32,32,896]{2,1,0:T(8,128)(2,1)} custom-call(bf16[32,8192]{1,0:T(8,128)(2,1)} %x_ref, bf16[32,8192]{1,0:T(8,128)(2,1)} %gy_ref.1, bf16[32,1024]{1,0:T(8,128)(2,1)} %b_ref.1, bf16[32,1024]{1,0:T(8,128)(2,1)} %c_ref.1, bf16[32,128]{1,0:T(8,128)(2,1)} %dt_ref.1), custom_call_target="tpu_custom_call" | custom-call | tf_op jit(solution)/shard_map/pallas_call | solution.py:86
  15.9 0.2 select_reduce_fusion
  16.1 9.5 %all-to-all-done = bf16[32,32,384]{2,1,0:T(8,128)(2,1)S(1)} async-done(((bf16[32,32,384]{2,1,0:T(8,128)(2,1)}), bf16[32,32,384]{2,1,0:T(8,128)(2,1)S(1)}, u32[]{:S(2)}, u32[]{:S(2)}) %all-to-all-start) | async-done | bytes 786464 | tf_op jit(solution)/shard_map/all_to_all | solution.py:571
  25.7 0.1 collective-permute-start.2
  25.8 0.0 collective-permute-done.3
  25.8 0.1 constant_dynamic-slice_fusion
  25.9 6.4 %collective-permute-start.1 = (bf16[1024,128]{1,0:T(8,128)(2,1)S(1)}, bf16[1024,128]{1,0:T(8,128)(2,1)}, u32[]{:S(2)}, u32[]{:S(2)}) collective-permute-start(bf16[1024,128]{1,0:T(8,128)(2,1)S(1)} %slice.16.own0), channel_id=1, source_target_pairs={{0,64},{32,96},{64,128},{96,160},{128,192},{160,224},{1,65},{33,97... | collective-permute-start | bytes 786440 | tf_op jit(solution)/shard_map/ppermute | solution.py:567
  32.2 2.9 %collective-permute-start = (bf16[1024,128]{1,0:T(8,128)(2,1)S(1)}, bf16[1024,128]{1,0:T(8,128)(2,1)}, u32[]{:S(2)}, u32[]{:S(2)}) collective-permute-start(bf16[1024,128]{1,0:T(8,128)(2,1)S(1)} %slice.16.own0), channel_id=1, source_target_pairs={{0,32},{32,64},{64,96},{96,128},{128,160},{160,192},{192,224},{1,3... | collective-permute-start | bytes 786440 | tf_op jit(solution)/shard_map/ppermute | solution.py:567
  35.2 0.0 collective-permute-done.2.oth0
  35.2 4.1 %all-to-all-start.1 = ((bf16[32,32,896]{2,1,0:T(8,128)(2,1)}), bf16[32,32,896]{2,1,0:T(8,128)(2,1)S(1)}, u32[]{:S(2)}, u32[]{:S(2)}) async-start(bf16[32,32,896]{2,1,0:T(8,128)(2,1)} %shard_map.180), calls=%async_computation.1 | async-start | bytes 3670016 | tf_op jit(solution)/shard_map/all_to_all | solution.py:571
  39.3 5.2 %collective-permute-done.1.own2 = bf16[1024,128]{1,0:T(8,128)(2,1)} collective-permute-done((bf16[1024,128]{1,0:T(8,128)(2,1)S(1)}, bf16[1024,128]{1,0:T(8,128)(2,1)}, u32[]{:S(2)}, u32[]{:S(2)}) %collective-permute-start.1) | collective-permute-done | bytes 262176 | tf_op jit(solution)/shard_map/ppermute | solution.py:567
  44.5 0.0 collective-permute-start.5
  44.5 5.2 %collective-permute-done.own1 = bf16[1024,128]{1,0:T(8,128)(2,1)} collective-permute-done((bf16[1024,128]{1,0:T(8,128)(2,1)S(1)}, bf16[1024,128]{1,0:T(8,128)(2,1)}, u32[]{:S(2)}, u32[]{:S(2)}) %collective-permute-start) | collective-permute-done | bytes 262176 | tf_op jit(solution)/shard_map/ppermute | solution.py:567
  49.7 0.0 collective-permute-start.4
  49.7 0.1 slice.15
  49.8 0.0 collective-permute-done.5.oth2
  49.8 1.8 %collective-permute-done.4.oth1 = bf16[1024,128]{1,0:T(8,128)(2,1)} collective-permute-done((bf16[1024,128]{1,0:T(8,128)(2,1)}, bf16[1024,128]{1,0:T(8,128)(2,1)}, u32[]{:S(2)}, u32[]{:S(2)}) %collective-permute-start.4) | collective-permute-done | bytes 262176 | tf_op jit(solution)/shard_map/ppermute | solution.py:575
  51.5 9.0 %shard_map.181 = (bf16[1024,256]{1,0:T(8,128)(2,1)}, bf16[3072,128]{1,0:T(8,128)(2,1)}, bf16[3072,128]{1,0:T(8,128)(2,1)}) custom-call(s32[1]{0:T(128)} %bitcast.core, s32[1024]{0:T(1024)S(1)} %broadcast_subtract_fusion.starts, bf16[1024,384]{1,0:T(8,128)(2,1)S(1)} %bitcast.27, bf16[1024,128]{1,0:T(8,128)(2,1)S(1)} %slice.16.own0, ...), custom_call_target="tpu_custom_call" | custom-call | flops 5000000000 | bytes 1000000 | tf_op jit(solution)/shard_map/pallas_call | solution.py:538
  60.6 0.2 collective-permute-start.6
  60.8 0.1 pad.3.clone
  60.9 0.2 select_reduce_fusion.2
  61.1 0.1 bitcast_subtract_fusion.ends_ref
  61.2 2.0 %collective-permute-done.6.come_ref = bf16[3072,128]{1,0:T(8,128)(2,1)S(1)} collective-permute-done((bf16[3072,128]{1,0:T(8,128)(2,1)}, bf16[3072,128]{1,0:T(8,128)(2,1)S(1)}, u32[]{:S(2)}, u32[]{:S(2)}) %collective-permute-start.6) | collective-permute-done | bytes 786464 | tf_op jit(solution)/shard_map/ppermute | solution.py:575
  63.2 2.6 %shard_map.182 = bf16[1024,640]{1,0:T(8,128)(2,1)} custom-call(bf16[1024,256]{1,0:T(8,128)(2,1)} %get-tuple-element.50.att_ref, bf16[3072,128]{1,0:T(8,128)(2,1)} %get-tuple-element.51.keep_ref, bf16[3072,128]{1,0:T(8,128)(2,1)S(1)} %collective-permute-done.6.come_ref), custom_call_target="tpu_custom_call" | custom-call | tf_op jit(solution)/shard_map/pallas_call | solution.py:194
  65.8 0.0 all-to-all-done.1
  65.8 4.2 %all-to-all-start.2 = ((bf16[32,32,640]{2,1,0:T(8,128)(2,1)}), bf16[32,32,640]{2,1,0:T(8,128)(2,1)S(1)}, u32[]{:S(2)}, u32[]{:S(2)}) async-start(bf16[32,32,640]{2,1,0:T(8,128)(2,1)} %bitcast.29), calls=%async_computation.2 | async-start | bytes 2621440 | tf_op jit(solution)/shard_map/all_to_all | solution.py:571
  70.0 0.1 add_add_fusion.info
  70.1 2.8 %shard_map.183 = (f32[8,128,256]{2,1,0:T(8,128)S(1)}, f32[8,128,256]{2,1,0:T(8,128)S(1)}, f32[16,256]{1,0:T(8,128)S(1)}, bf16[144,256]{1,0:T(8,128)(2,1)S(1)}, b...) custom-call(s32[4,8]{1,0:T(4,128)S(1)} %add_add_fusion.info, ...), custom_call_target="tpu_custom_call" | custom-call | flops 3000000000 | bytes 1000000 | tf_op jit(solution)/shard_map/pallas_call | solution.py:287
  72.9 13.6 %collective-permute-start.8 = (bf16[144,256]{1,0:T(8,128)(2,1)S(1)}, bf16[144,256]{1,0:T(8,128)(2,1)S(1)}, u32[]{:S(2)}, u32[]{:S(2)}) collective-permute-start(bf16[144,256]{1,0:T(8,128)(2,1)S(1)} %get-tuple-element.64), channel_id=1, source_target_pairs={{0,64},{32,96},{64,128},{96,160},{128,192},{160,224},{1,65},{33,97... | collective-permute-start | bytes 221192 | tf_op jit(solution)/shard_map/ppermute | solution.py:567
  86.6 1.9 %collective-permute-start.7 = (bf16[144,256]{1,0:T(8,128)(2,1)S(1)}, bf16[144,256]{1,0:T(8,128)(2,1)S(1)}, u32[]{:S(2)}, u32[]{:S(2)}) collective-permute-start(bf16[144,256]{1,0:T(8,128)(2,1)S(1)} %get-tuple-element.64), channel_id=1, source_target_pairs={{0,32},{32,64},{64,96},{96,128},{128,160},{160,192},{192,224},{1,3... | collective-permute-start | bytes 221192 | tf_op jit(solution)/shard_map/ppermute | solution.py:567
  88.5 1.9 %collective-permute-start.10 = (bf16[144,256]{1,0:T(8,128)(2,1)S(1)}, bf16[144,256]{1,0:T(8,128)(2,1)S(1)}, u32[]{:S(2)}, u32[]{:S(2)}) collective-permute-start(bf16[144,256]{1,0:T(8,128)(2,1)S(1)} %get-tuple-element.65), channel_id=1, source_target_pairs={{64,0},{96,32},{128,64},{160,96},{192,128},{224,160},{65,1},{97,33... | collective-permute-start | bytes 221192 | tf_op jit(solution)/shard_map/ppermute | solution.py:567
  90.4 3.3 %collective-permute-start.9 = (bf16[144,256]{1,0:T(8,128)(2,1)S(1)}, bf16[144,256]{1,0:T(8,128)(2,1)S(1)}, u32[]{:S(2)}, u32[]{:S(2)}) collective-permute-start(bf16[144,256]{1,0:T(8,128)(2,1)S(1)} %get-tuple-element.65), channel_id=1, source_target_pairs={{32,0},{64,32},{96,64},{128,96},{160,128},{192,160},{224,192},{33,... | collective-permute-start | bytes 221192 | tf_op jit(solution)/shard_map/ppermute | solution.py:567
  93.7 7.6 %shard_map.184.part_ref = f32[1024,768]{1,0:T(8,128)S(1)} custom-call(s32[4,8]{1,0:T(4,128)S(1)} %add_add_fusion.info, f32[4]{0:T(128)S(1)} %get-tuple-element.55.rates, f32[4]{0:T(128)S(1)} %get-tuple-element.58.skips, bf16[1024,896]{1,0:T(8,128)(2,1)S(1)} %bitcast.24, s32[8,128]{1,0:T(8,128)S(1)} %bitcast_subtract_fusion.ends_ref), custom_call_target="tpu_custom_call" | custom-call | flops 8000000000 | bytes 1000000 | tf_op jit(solution)/shard_map/pallas_call | solution.py:369
  101.4 0.0 collective-permute-done.8.f2
  101.4 0.0 collective-permute-done.7.f1
  101.4 0.0 collective-permute-done.10.b2
  101.4 0.0 collective-permute-done.9.b1
  101.4 1.9 %shard_map.185 = bf16[1024,768]{1,0:T(8,128)(2,1)} custom-call(bf16[1024,896]{1,0:T(8,128)(2,1)S(1)} %bitcast.25, f32[1024,768]{1,0:T(8,128)S(1)} %shard_map.184.part_ref, bf16[1024,512]{1,0:T(8,128)(2,1)S(1)} %get-tuple-element.59.low_ref, f32[1024,512]{1,0:T(8,128)S(1)} %get-tuple-element.60.full_ref, f32[8,128,256]{2,1,0:T(8,128)S(1)} %get-tuple-element.61.inc_ref, ...), custom_call_target="tpu_custom_call" | custom-call | flops 2000000000 | bytes 1000000 | tf_op jit(solution)/shard_map/pallas_call | solution.py:401
  103.3 0.0 all-to-all-done.2.in_ref
  103.3 7.2 %all-to-all-start.3 = ((bf16[32,32,768]{2,1,0:T(8,128)(2,1)}), bf16[32,32,768]{2,1,0:T(8,128)(2,1)S(1)}, u32[]{:S(2)}, u32[]{:S(2)}) async-start(bf16[32,32,768]{2,1,0:T(8,128)(2,1)} %bitcast.28), calls=%async_computation.3 | async-start | bytes 3145728 | tf_op jit(solution)/shard_map/all_to_all | solution.py:571
  110.6 1.5 %shard_map.187 = (bf16[32,4096]{1,0:T(8,128)(2,1)}, bf16[32,4096]{1,0:T(8,128)(2,1)}, bf16[32,2048]{1,0:T(8,128)(2,1)S(1)}, bf16[32,2048]{1,0:T(8,128)(2,1)S(1)}, f32[32,2048]{1,0:T(8,128)S(1)}) custom-call(bf16[32,32,640]{2,1,0:T(8,128)(2,1)S(1)} %all-to-all-done.2.in_ref), custom_call_target="tpu_custom_call" | custom-call | tf_op jit(solution)/shard_map/pallas_call | solution.py:151
  112.0 1.9 %collective-permute-start.11 = (bf16[32,2048]{1,0:T(8,128)(2,1)S(1)}, bf16[32,2048]{1,0:T(8,128)(2,1)S(1)}, u32[]{:S(2)}, u32[]{:S(2)}) collective-permute-start(bf16[32,2048]{1,0:T(8,128)(2,1)S(1)} %get-tuple-element.76), channel_id=1, source_target_pairs={{32,0},{64,32},{96,64},{128,96},{160,128},{192,160},{224,192},{33,... | collective-permute-start | bytes 393224 | tf_op jit(solution)/shard_map/ppermute | solution.py:567
  113.9 1.9 %collective-permute-start.12 = (bf16[32,2048]{1,0:T(8,128)(2,1)S(1)}, bf16[32,2048]{1,0:T(8,128)(2,1)S(1)}, u32[]{:S(2)}, u32[]{:S(2)}) collective-permute-start(bf16[32,2048]{1,0:T(8,128)(2,1)S(1)} %get-tuple-element.77), channel_id=1, source_target_pairs={{64,0},{96,32},{128,64},{160,96},{192,128},{224,160},{65,1},{97,33... | collective-permute-start | bytes 393224 | tf_op jit(solution)/shard_map/ppermute | solution.py:567
  115.9 4.4 %collective-permute-done.11.one_ref = bf16[32,2048]{1,0:T(8,128)(2,1)S(1)} collective-permute-done((bf16[32,2048]{1,0:T(8,128)(2,1)S(1)}, bf16[32,2048]{1,0:T(8,128)(2,1)S(1)}, u32[]{:S(2)}, u32[]{:S(2)}) %collective-permute-start.11) | collective-permute-done | bytes 131104 | tf_op jit(solution)/shard_map/ppermute | solution.py:567
  120.3 8.0 %collective-permute-done.12.two_ref = bf16[32,2048]{1,0:T(8,128)(2,1)S(1)} collective-permute-done((bf16[32,2048]{1,0:T(8,128)(2,1)S(1)}, bf16[32,2048]{1,0:T(8,128)(2,1)S(1)}, u32[]{:S(2)}, u32[]{:S(2)}) %collective-permute-start.12) | collective-permute-done | bytes 131104 | tf_op jit(solution)/shard_map/ppermute | solution.py:567
  128.2 0.7 shard_map.188
  128.9 4.1 %all-to-all-done.3.in_ref = bf16[32,32,768]{2,1,0:T(8,128)(2,1)S(1)} async-done(((bf16[32,32,768]{2,1,0:T(8,128)(2,1)}), bf16[32,32,768]{2,1,0:T(8,128)(2,1)S(1)}, u32[]{:S(2)}, u32[]{:S(2)}) %all-to-all-start.3) | async-done | bytes 1572896 | tf_op jit(solution)/shard_map/all_to_all | solution.py:571
  133.0 1.6 %shard_map.186 = (bf16[32,8192]{1,0:T(8,128)(2,1)}, bf16[32,8192]{1,0:T(8,128)(2,1)}, bf16[32,1024]{1,0:T(8,128)(2,1)}, bf16[32,1024]{1,0:T(8,128)(2,1)}) custom-call(bf16[32,32,768]{2,1,0:T(8,128)(2,1)S(1)} %all-to-all-done.3.in_ref), custom_call_target="tpu_custom_call" | custom-call | tf_op jit(solution)/shard_map/pallas_call | solution.py:120
  (11 shorter events, 0.1 us)
Async XLA Ops:
  0.6 10.6 %copy-start.2 = (f32[32]{0:T(128)S(1)}, f32[32]{0:T(128)}, u32[]{:S(2)}) copy-start(f32[32]{0:T(128)} %param.16) | copy-start | bytes 388
  0.6 10.6 %copy-start.1 = (f32[32]{0:T(128)S(1)}, f32[32]{0:T(128)}, u32[]{:S(2)}) copy-start(f32[32]{0:T(128)} %param.17) | copy-start | bytes 388
  0.7 11.3 %copy-start = (s32[64]{0:T(128)S(1)}, s32[64]{0:T(128)}, u32[]{:S(2)}) copy-start(s32[64]{0:T(128)} %param.21) | copy-start | bytes 772
  3.9 21.7 %all-to-all-start = ((bf16[32,32,384]{2,1,0:T(8,128)(2,1)}), bf16[32,32,384]{2,1,0:T(8,128)(2,1)S(1)}, u32[]{:S(2)}, u32[]{:S(2)}) async-start(bf16[32,32,384]{2,1,0:T(8,128)(2,1)} %shard_map.179), calls=%async_computation | async-start | bytes 1572864 | tf_op jit(solution)/shard_map/all_to_all | solution.py:571
  11.3 14.5 %collective-permute-start.3 = (f32[2,32]{1,0:T(2,128)S(1)}, f32[2,32]{1,0:T(2,128)S(1)}, u32[]{:S(2)}, u32[]{:S(2)}) collective-permute-start(f32[2,32]{1,0:T(2,128)S(1)} %pad_maximum_fusion), channel_id=1, source_target_pairs={{0,0},{1,8},{2,16},{3,24},{8,1},{9,9},{10,17},{11,25},{16,2},{17,1... | collective-permute-start | bytes 776 | tf_op jit(solution)/shard_map/ppermute | solution.py:587
  25.7 9.5 %collective-permute-start.2 = (bf16[1024,128]{1,0:T(8,128)(2,1)S(1)}, bf16[1024,128]{1,0:T(8,128)(2,1)S(1)}, u32[]{:S(2)}, u32[]{:S(2)}) collective-permute-start(bf16[1024,128]{1,0:T(8,128)(2,1)S(1)} %slice.16.own0), channel_id=1, source_target_pairs={{0,4},{4,0},{1,5},{5,1},{2,6},{6,2},{3,7},{7,3},{8,12},{12,8},{9,1... | collective-permute-start | bytes 786440 | tf_op jit(solution)/shard_map/ppermute | solution.py:575
  25.9 18.6 %collective-permute-start.1 = (bf16[1024,128]{1,0:T(8,128)(2,1)S(1)}, bf16[1024,128]{1,0:T(8,128)(2,1)}, u32[]{:S(2)}, u32[]{:S(2)}) collective-permute-start(bf16[1024,128]{1,0:T(8,128)(2,1)S(1)} %slice.16.own0), channel_id=1, source_target_pairs={{0,64},{32,96},{64,128},{96,160},{128,192},{160,224},{1,65},{33,97... | collective-permute-start | bytes 786440 | tf_op jit(solution)/shard_map/ppermute | solution.py:567
  32.2 17.4 %collective-permute-start = (bf16[1024,128]{1,0:T(8,128)(2,1)S(1)}, bf16[1024,128]{1,0:T(8,128)(2,1)}, u32[]{:S(2)}, u32[]{:S(2)}) collective-permute-start(bf16[1024,128]{1,0:T(8,128)(2,1)S(1)} %slice.16.own0), channel_id=1, source_target_pairs={{0,32},{32,64},{64,96},{96,128},{128,160},{160,192},{192,224},{1,3... | collective-permute-start | bytes 786440 | tf_op jit(solution)/shard_map/ppermute | solution.py:567
  35.2 30.6 %all-to-all-start.1 = ((bf16[32,32,896]{2,1,0:T(8,128)(2,1)}), bf16[32,32,896]{2,1,0:T(8,128)(2,1)S(1)}, u32[]{:S(2)}, u32[]{:S(2)}) async-start(bf16[32,32,896]{2,1,0:T(8,128)(2,1)} %shard_map.180), calls=%async_computation.1 | async-start | bytes 3670016 | tf_op jit(solution)/shard_map/all_to_all | solution.py:571
  44.5 5.3 %collective-permute-start.5 = (bf16[1024,128]{1,0:T(8,128)(2,1)}, bf16[1024,128]{1,0:T(8,128)(2,1)}, u32[]{:S(2)}, u32[]{:S(2)}) collective-permute-start(bf16[1024,128]{1,0:T(8,128)(2,1)} %collective-permute-done.1.own2), channel_id=1, source_target_pairs={{0,4},{4,0},{1,5},{5,1},{2,6},{6,2},{3,7},{7,3},{8,12},{12,8},{9,1... | collective-permute-start | bytes 786440 | tf_op jit(solution)/shard_map/ppermute | solution.py:575
  49.7 1.9 %collective-permute-start.4 = (bf16[1024,128]{1,0:T(8,128)(2,1)}, bf16[1024,128]{1,0:T(8,128)(2,1)}, u32[]{:S(2)}, u32[]{:S(2)}) collective-permute-start(bf16[1024,128]{1,0:T(8,128)(2,1)} %collective-permute-done.own1), channel_id=1, source_target_pairs={{0,4},{4,0},{1,5},{5,1},{2,6},{6,2},{3,7},{7,3},{8,12},{12,8},{9,1... | collective-permute-start | bytes 786440 | tf_op jit(solution)/shard_map/ppermute | solution.py:575
  60.6 2.6 %collective-permute-start.6 = (bf16[3072,128]{1,0:T(8,128)(2,1)}, bf16[3072,128]{1,0:T(8,128)(2,1)S(1)}, u32[]{:S(2)}, u32[]{:S(2)}) collective-permute-start(bf16[3072,128]{1,0:T(8,128)(2,1)} %get-tuple-element.52), channel_id=1, source_target_pairs={{0,4},{4,0},{1,5},{5,1},{2,6},{6,2},{3,7},{7,3},{8,12},{12,8},{9,1... | collective-permute-start | bytes 2359304 | tf_op jit(solution)/shard_map/ppermute | solution.py:575
  65.8 37.6 %all-to-all-start.2 = ((bf16[32,32,640]{2,1,0:T(8,128)(2,1)}), bf16[32,32,640]{2,1,0:T(8,128)(2,1)S(1)}, u32[]{:S(2)}, u32[]{:S(2)}) async-start(bf16[32,32,640]{2,1,0:T(8,128)(2,1)} %bitcast.29), calls=%async_computation.2 | async-start | bytes 2621440 | tf_op jit(solution)/shard_map/all_to_all | solution.py:571
  72.9 28.4 %collective-permute-start.8 = (bf16[144,256]{1,0:T(8,128)(2,1)S(1)}, bf16[144,256]{1,0:T(8,128)(2,1)S(1)}, u32[]{:S(2)}, u32[]{:S(2)}) collective-permute-start(bf16[144,256]{1,0:T(8,128)(2,1)S(1)} %get-tuple-element.64), channel_id=1, source_target_pairs={{0,64},{32,96},{64,128},{96,160},{128,192},{160,224},{1,65},{33,97... | collective-permute-start | bytes 221192 | tf_op jit(solution)/shard_map/ppermute | solution.py:567
  86.6 14.8 %collective-permute-start.7 = (bf16[144,256]{1,0:T(8,128)(2,1)S(1)}, bf16[144,256]{1,0:T(8,128)(2,1)S(1)}, u32[]{:S(2)}, u32[]{:S(2)}) collective-permute-start(bf16[144,256]{1,0:T(8,128)(2,1)S(1)} %get-tuple-element.64), channel_id=1, source_target_pairs={{0,32},{32,64},{64,96},{96,128},{128,160},{160,192},{192,224},{1,3... | collective-permute-start | bytes 221192 | tf_op jit(solution)/shard_map/ppermute | solution.py:567
  88.5 12.9 %collective-permute-start.10 = (bf16[144,256]{1,0:T(8,128)(2,1)S(1)}, bf16[144,256]{1,0:T(8,128)(2,1)S(1)}, u32[]{:S(2)}, u32[]{:S(2)}) collective-permute-start(bf16[144,256]{1,0:T(8,128)(2,1)S(1)} %get-tuple-element.65), channel_id=1, source_target_pairs={{64,0},{96,32},{128,64},{160,96},{192,128},{224,160},{65,1},{97,33... | collective-permute-start | bytes 221192 | tf_op jit(solution)/shard_map/ppermute | solution.py:567
  90.4 11.0 %collective-permute-start.9 = (bf16[144,256]{1,0:T(8,128)(2,1)S(1)}, bf16[144,256]{1,0:T(8,128)(2,1)S(1)}, u32[]{:S(2)}, u32[]{:S(2)}) collective-permute-start(bf16[144,256]{1,0:T(8,128)(2,1)S(1)} %get-tuple-element.65), channel_id=1, source_target_pairs={{32,0},{64,32},{96,64},{128,96},{160,128},{192,160},{224,192},{33,... | collective-permute-start | bytes 221192 | tf_op jit(solution)/shard_map/ppermute | solution.py:567
  103.3 29.7 %all-to-all-start.3 = ((bf16[32,32,768]{2,1,0:T(8,128)(2,1)}), bf16[32,32,768]{2,1,0:T(8,128)(2,1)S(1)}, u32[]{:S(2)}, u32[]{:S(2)}) async-start(bf16[32,32,768]{2,1,0:T(8,128)(2,1)} %bitcast.28), calls=%async_computation.3 | async-start | bytes 3145728 | tf_op jit(solution)/shard_map/all_to_all | solution.py:571
  112.0 8.2 %collective-permute-start.11 = (bf16[32,2048]{1,0:T(8,128)(2,1)S(1)}, bf16[32,2048]{1,0:T(8,128)(2,1)S(1)}, u32[]{:S(2)}, u32[]{:S(2)}) collective-permute-start(bf16[32,2048]{1,0:T(8,128)(2,1)S(1)} %get-tuple-element.76), channel_id=1, source_target_pairs={{32,0},{64,32},{96,64},{128,96},{160,128},{192,160},{224,192},{33,... | collective-permute-start | bytes 393224 | tf_op jit(solution)/shard_map/ppermute | solution.py:567
  113.9 14.3 %collective-permute-start.12 = (bf16[32,2048]{1,0:T(8,128)(2,1)S(1)}, bf16[32,2048]{1,0:T(8,128)(2,1)S(1)}, u32[]{:S(2)}, u32[]{:S(2)}) collective-permute-start(bf16[32,2048]{1,0:T(8,128)(2,1)S(1)} %get-tuple-element.77), channel_id=1, source_target_pairs={{64,0},{96,32},{128,64},{160,96},{192,128},{224,160},{65,1},{97,33... | collective-permute-start | bytes 393224 | tf_op jit(solution)/shard_map/ppermute | solution.py:567

commit v3 on v2

--- a/solution.py
+++ b/solution.py
@@ -21,7 +21,7 @@
 TQ = 512
 TK = 512
 UNROLL = 2
-ATT = 5
+ATT = 3.5
 NEG = -1e30
 NN = (((1,), (0,)), ((), ()))
 NT = (((1,), (1,)), ((), ()))
@@ -464,59 +464,64 @@
         s = jnp.where((at + diag[i] >= begins[i]) & (at <= here), s, NEG)
         peak = jnp.max(s, axis=0, keepdims=True)
         p = jnp.exp((s - peak) * SCALE)
-        near_ref[i] = p
+        p_low = p.astype(BF)
+        near_ref[i] = p_low
         peak_ref[i, 4:5, :] = peak
-        carries.append((peak, tile_sum(p), dot(vt_ref[:, near[i]], p.astype(BF))))
-
-    for i in range(count):
-        q = in_ref[q_rows[i], 0:128]
-
-        def forward(t, carry):
-            peak, total, att = carry
-            base = diag[i] - TK * (t + 1)
-            rows = pl.ds(pl.multiple_of(base, TQ), TK)
-            s = dot(k_ref[rows, :], q, NT)
-            s = jnp.where(far_at >= begins[i] - base, s, NEG)
-            top = jnp.maximum(peak, jnp.max(s, axis=0, keepdims=True))
-            alpha = jnp.exp((peak - top) * SCALE)
-            p = jnp.exp((s - top) * SCALE)
-            far_ref[i, t] = p
-            peak_ref[i, pl.ds(t, 1), :] = top
-            att = att * alpha + dot(vt_ref[:, rows], p.astype(BF))
-            return top, total * alpha + tile_sum(p), att
-
-        carries[i] = lax.fori_loop(0, many[i], forward, carries[i])
+        carries.append((peak, tile_sum(p), dot(vt_ref[:, near[i]], p_low)))
+
+    def forward(i, t, carry):
+        peak, total, att = carry
+        base = diag[i] - TK * (t + 1)
+        rows = pl.ds(pl.multiple_of(base, TQ), TK)
+        s = dot(k_ref[rows, :], in_ref[q_rows[i], 0:128], NT)
+        s = jnp.where(far_at >= begins[i] - base, s, NEG)
+        top = jnp.maximum(peak, jnp.max(s, axis=0, keepdims=True))
+        alpha = jnp.exp((peak - top) * SCALE)
+        p = jnp.exp((s - top) * SCALE)
+        p_low = p.astype(BF)
+        far_ref[i, t] = p_low
+        peak_ref[i, pl.ds(t, 1), :] = top
+        att = att * alpha + dot(vt_ref[:, rows], p_low)
+        return top, total * alpha + tile_sum(p), att
+
+    def paired(step, carries):
+        shared = many[0]
+        for other in many[1:]:
+            shared = jnp.minimum(shared, other)
+        carries = lax.fori_loop(
+            0, shared, lambda t, c: tuple(step(i, t, c[i]) for i in range(count)), tuple(carries)
+        )
+        return [
+            lax.fori_loop(shared, many[i], lambda t, c, i=i: step(i, t, c), carries[i])
+            for i in range(count)
+        ]
+
+    carries = paired(forward, carries)
+
+    def grads(i, t, rows, p_low, peak, inverse, delta, ga_turned):
+        factor = jnp.exp((peak_ref[i, pl.ds(t, 1), :] - peak) * SCALE) * inverse
+        ga = (ga_turned * factor).astype(BF)
+        ds = (p_low.astype(F32) * (dot(v_ref[rows, :], ga) - delta * factor)).astype(BF)
+        gk_ref[rows, :] += dot(ds, in_ref[q_rows[i], 0:128])
+        gv_ref[rows, :] += dot(p_low, ga, NT)
+        return dot(kt_ref[:, rows], ds)
 
     rest = []
     for i in range(count):
         peak, total, att = carries[i]
-        q = in_ref[q_rows[i], 0:128]
-        ga = in_ref[q_rows[i], 128:256]
+        ga_turned = in_ref[q_rows[i], 128:256].T.astype(F32)
         inverse = 1.0 / jnp.sum(total, axis=0, keepdims=True)
         att = (att * inverse).astype(BF)
         out_ref[q_rows[i], 0:128] = att.T
-        delta = jnp.sum(ga.T.astype(F32) * att.astype(F32), axis=0, keepdims=True)
-        probs = near_ref[i] * (jnp.exp((peak_ref[i, 4:5, :] - peak) * SCALE) * inverse)
-        ds = (probs * (dot(v_ref[near[i], :], ga, NT) - delta)).astype(BF)
-        gk_ref[near[i], :] += dot(ds, q)
-        gv_ref[near[i], :] += dot(probs.astype(BF), ga)
-        rest.append((peak, inverse, delta, dot(kt_ref[:, near[i]], ds)))
-
-    for i in range(count):
-        peak, inverse, delta, gq = rest[i]
-        q = in_ref[q_rows[i], 0:128]
-        ga = in_ref[q_rows[i], 128:256]
-
-        def backward(t, gq):
-            rows = pl.ds(pl.multiple_of(diag[i] - TK * (t + 1), TQ), TK)
-            factor = jnp.exp((peak_ref[i, pl.ds(t, 1), :] - peak) * SCALE) * inverse
-            probs = far_ref[i, t] * factor
-            ds = (probs * (dot(v_ref[rows, :], ga, NT) - delta)).astype(BF)
-            gk_ref[rows, :] += dot(ds, q)
-            gv_ref[rows, :] += dot(probs.astype(BF), ga)
-            return gq + dot(kt_ref[:, rows], ds)
-
-        gq = lax.fori_loop(0, many[i], backward, gq)
+        delta = jnp.sum(ga_turned * att.astype(F32), axis=0, keepdims=True)
+        state = (peak, inverse, delta, ga_turned)
+        rest.append((state, grads(i, 4, near[i], near_ref[i], *state)))
+
+    def backward(i, t, gq):
+        rows = pl.ds(pl.multiple_of(diag[i] - TK * (t + 1), TQ), TK)
+        return gq + grads(i, t, rows, far_ref[i, t], *rest[i][0])
+
+    for i, gq in enumerate(paired(backward, [gq for _, gq in rest])):
         out_ref[q_rows[i], 128:256] = (gq * SCALE).astype(BF).T
 
     def store(k_out, v_out):
@@ -549,8 +554,8 @@
             pltpu.VMEM((span, 128), BF),
             pltpu.VMEM((128, span), BF),
             pltpu.VMEM((128, span), BF),
-            pltpu.VMEM((count, TQ, TQ), F32),
-            pltpu.VMEM((count, 4, TK, TQ), F32),
+            pltpu.VMEM((count, TQ, TQ), BF),
+            pltpu.VMEM((count, 4, TK, TQ), BF),
             pltpu.VMEM((count, 8, TQ), F32),
             pltpu.VMEM((span, 128), F32),
             pltpu.VMEM((span, 128), F32),
@@ -619,7 +624,8 @@
     got_a, packed_m = lax.optimization_barrier((exchange(packed_a), packed_m))
     got_a = got_a.reshape(SUPER, 384)
     own0 = got_a[:, 256:384]
-    own1, own2 = shifted(own0, 1), shifted(own0, 2)
+    own1 = shifted(own0, 1)
+    own2 = shifted(own1, 1)
     oth0 = swapped(own0)
     packed_m, oth0, my_rates, my_skips = lax.optimization_barrier(
         (packed_m, oth0, my_rates, my_skips)

time: 135 us -> 131 us (0.970); the launches traced: 135 us -> 129 us
  starting transfers between devices: 57.7 us -> 54 us
  waiting for transfers between devices: 40.2 us -> 38.1 us
    ppermute x8, starting transfers between devices: 33.9 us -> 28.2 us  [shifted(): return lax.ppermute(block, 'z', route)]
    ppermute x8, waiting for transfers between devices: 22.7 us -> 20.2 us  [shifted(): return lax.ppermute(block, 'z', route)]
    all_to_all x4, starting transfers between devices: 22.8 us -> 24.5 us  [exchange(): return lax.all_to_all(block, GROUP, split_axis=0, concat_axis=0, tiled=True)]
  transfers between devices with their start and end apart: 17 -> 17, of which waited for: 8 -> 8; matrix products, arithmetic and copies ran while one was open for 1% -> 1% of each run, Pallas kernels for 22% -> 23%
where the time goes in v3:
time: 131 us; the launch traced here: 129 us
  starting transfers between devices  54 us (41%)
  waiting for transfers between devices  38.1 us (29%)
  Pallas kernels  34.4 us (26%)
    ppermute x8, starting transfers between devices, shifted(): return lax.ppermute(block, 'z', route)  28.2 us
    all_to_all x4, starting transfers between devices, exchange(): return lax.all_to_all(block, GROUP, split_axis=0, concat_axis=0, tiled=True)  24.5 us
    ppermute x8, waiting for transfers between devices, shifted(): return lax.ppermute(block, 'z', route)  20.2 us
    all_to_all x4, waiting for transfers between devices, exchange(): return lax.all_to_all(block, GROUP, split_axis=0, concat_axis=0, tiled=True)  14.2 us
    pallas_call x1, Pallas kernels, do_attention(): pl.pallas_call(attention_kernel, in_specs=[smem()] * 2 + [vmem()] + [pl.B...  8.83 us
    pallas_call x1, Pallas kernels, do_inner(): pl.pallas_call(inner_kernel, in_specs=[smem()] * 3 + [vmem()] * 2, out_sp...  7.64 us
    ppermute x4, waiting for transfers between devices, swapped(): return lax.ppermute(block, 'core', [(0, 1), (1, 0)])  3.75 us
    pallas_call x1, Pallas kernels, do_pack_mixer(): pl.pallas_call(pack_mixer, grid=(4,), in_specs=[wide(2048), wide(2048), w...  3.64 us
  transfers between devices with their start and end apart: 17, of which 8 were waited for; matrix products, arithmetic and copies ran while one was open for 1% of the time, Pallas kernels for 23%

profile of v3, /device:TPU:64, one launch (start us, length us, event | category | flops | bytes accessed | tf_op | source)
XLA Modules:
  0.0 128.7 jit_solution(2133214176442052541)
XLA Ops:
  0.6 0.0 copy-start.2
  0.6 0.0 copy-start.1
  0.7 0.0 copy-start
  0.7 3.2 %shard_map.179 = bf16[32,32,384]{2,1,0:T(8,128)(2,1)} custom-call(bf16[32,4096]{1,0:T(8,128)(2,1)} %q_ref.1, bf16[32,4096]{1,0:T(8,128)(2,1)} %ga_ref.1, bf16[32,1024]{1,0:T(8,128)(2,1)} %k_ref.1, bf16[32,1024]{1,0:T(8,128)(2,1)} %v_ref.1), custom_call_target="tpu_custom_call" | custom-call | tf_op jit(solution)/shard_map/pallas_call | solution.py:97
  3.9 7.3 %all-to-all-start = ((bf16[32,32,384]{2,1,0:T(8,128)(2,1)}), bf16[32,32,384]{2,1,0:T(8,128)(2,1)S(1)}, u32[]{:S(2)}, u32[]{:S(2)}) async-start(bf16[32,32,384]{2,1,0:T(8,128)(2,1)} %shard_map.179), calls=%async_computation | async-start | bytes 1572864 | tf_op jit(solution)/shard_map/all_to_all | solution.py:576
  11.2 0.0 copy-done.2
  11.2 0.0 copy-done.1
  11.3 0.7 collective-permute-start.3
  12.0 0.0 copy-done
  12.0 0.1 copy.22
  12.1 0.1 reduce-window.8
  12.2 0.1 reduce
  12.3 3.6 %shard_map.180 = bf16[32,32,896]{2,1,0:T(8,128)(2,1)} custom-call(bf16[32,8192]{1,0:T(8,128)(2,1)} %x_ref, bf16[32,8192]{1,0:T(8,128)(2,1)} %gy_ref.1, bf16[32,1024]{1,0:T(8,128)(2,1)} %b_ref.1, bf16[32,1024]{1,0:T(8,128)(2,1)} %c_ref.1, bf16[32,128]{1,0:T(8,128)(2,1)} %dt_ref.1), custom_call_target="tpu_custom_call" | custom-call | tf_op jit(solution)/shard_map/pallas_call | solution.py:86
  15.9 9.7 %all-to-all-done = bf16[32,32,384]{2,1,0:T(8,128)(2,1)S(1)} async-done(((bf16[32,32,384]{2,1,0:T(8,128)(2,1)}), bf16[32,32,384]{2,1,0:T(8,128)(2,1)S(1)}, u32[]{:S(2)}, u32[]{:S(2)}) %all-to-all-start) | async-done | bytes 786464 | tf_op jit(solution)/shard_map/all_to_all | solution.py:576
  25.7 0.1 collective-permute-start.2
  25.8 3.8 %collective-permute-start = (bf16[1024,128]{1,0:T(8,128)(2,1)S(1)}, bf16[1024,128]{1,0:T(8,128)(2,1)}, u32[]{:S(2)}, u32[]{:S(2)}) collective-permute-start(bf16[1024,128]{1,0:T(8,128)(2,1)S(1)} %slice.16.own0), channel_id=1, source_target_pairs={{0,32},{32,64},{64,96},{96,128},{128,160},{160,192},{192,224},{1,3... | collective-permute-start | bytes 786440 | tf_op jit(solution)/shard_map/ppermute | solution.py:572
  29.6 0.0 collective-permute-done.3
  29.6 0.1 constant_dynamic-slice_fusion
  29.7 0.0 collective-permute-done.2.oth0
  29.7 4.0 %all-to-all-start.1 = ((bf16[32,32,896]{2,1,0:T(8,128)(2,1)}), bf16[32,32,896]{2,1,0:T(8,128)(2,1)S(1)}, u32[]{:S(2)}, u32[]{:S(2)}) async-start(bf16[32,32,896]{2,1,0:T(8,128)(2,1)} %shard_map.180), calls=%async_computation.1 | async-start | bytes 3670016 | tf_op jit(solution)/shard_map/all_to_all | solution.py:576
  33.8 2.7 %collective-permute-done.own1 = bf16[1024,128]{1,0:T(8,128)(2,1)} collective-permute-done((bf16[1024,128]{1,0:T(8,128)(2,1)S(1)}, bf16[1024,128]{1,0:T(8,128)(2,1)}, u32[]{:S(2)}, u32[]{:S(2)}) %collective-permute-start) | collective-permute-done | bytes 262176 | tf_op jit(solution)/shard_map/ppermute | solution.py:572
  36.5 4.4 %collective-permute-start.1 = (bf16[1024,128]{1,0:T(8,128)(2,1)}, bf16[1024,128]{1,0:T(8,128)(2,1)}, u32[]{:S(2)}, u32[]{:S(2)}) collective-permute-start(bf16[1024,128]{1,0:T(8,128)(2,1)} %collective-permute-done.own1), channel_id=1, source_target_pairs={{0,32},{32,64},{64,96},{96,128},{128,160},{160,192},{192,224},{1,3... | collective-permute-start | bytes 786440 | tf_op jit(solution)/shard_map/ppermute | solution.py:572
  40.8 0.2 select_reduce_fusion
  41.0 0.1 collective-permute-start.4
  41.1 5.5 %collective-permute-done.1.own2 = bf16[1024,128]{1,0:T(8,128)(2,1)} collective-permute-done((bf16[1024,128]{1,0:T(8,128)(2,1)}, bf16[1024,128]{1,0:T(8,128)(2,1)}, u32[]{:S(2)}, u32[]{:S(2)}) %collective-permute-start.1) | collective-permute-done | bytes 262176 | tf_op jit(solution)/shard_map/ppermute | solution.py:572
  46.6 0.0 collective-permute-start.5
  46.6 0.1 slice.15
  46.7 0.0 collective-permute-done.4.oth1
  46.7 1.8 %collective-permute-done.5.oth2 = bf16[1024,128]{1,0:T(8,128)(2,1)} collective-permute-done((bf16[1024,128]{1,0:T(8,128)(2,1)}, bf16[1024,128]{1,0:T(8,128)(2,1)}, u32[]{:S(2)}, u32[]{:S(2)}) %collective-permute-start.5) | collective-permute-done | bytes 262176 | tf_op jit(solution)/shard_map/ppermute | solution.py:580
  48.5 8.8 %shard_map.181 = (bf16[1024,256]{1,0:T(8,128)(2,1)}, bf16[3072,128]{1,0:T(8,128)(2,1)}, bf16[3072,128]{1,0:T(8,128)(2,1)}) custom-call(s32[1]{0:T(128)} %bitcast.core, s32[1024]{0:T(1024)S(1)} %broadcast_subtract_fusion.starts, bf16[1024,384]{1,0:T(8,128)(2,1)S(1)} %bitcast.27, bf16[1024,128]{1,0:T(8,128)(2,1)S(1)} %slice.16.own0, ...), custom_call_target="tpu_custom_call" | custom-call | flops 3500000000 | bytes 1000000 | tf_op jit(solution)/shard_map/pallas_call | solution.py:543
  57.3 0.4 collective-permute-start.6
  57.7 0.1 pad.3.clone
  57.8 0.2 select_reduce_fusion.2
  58.0 0.1 bitcast_subtract_fusion.ends_ref
  58.1 2.0 %collective-permute-done.6.come_ref = bf16[3072,128]{1,0:T(8,128)(2,1)S(1)} collective-permute-done((bf16[3072,128]{1,0:T(8,128)(2,1)}, bf16[3072,128]{1,0:T(8,128)(2,1)S(1)}, u32[]{:S(2)}, u32[]{:S(2)}) %collective-permute-start.6) | collective-permute-done | bytes 786464 | tf_op jit(solution)/shard_map/ppermute | solution.py:580
  60.1 2.6 %shard_map.182 = bf16[1024,640]{1,0:T(8,128)(2,1)} custom-call(bf16[1024,256]{1,0:T(8,128)(2,1)} %get-tuple-element.50.att_ref, bf16[3072,128]{1,0:T(8,128)(2,1)} %get-tuple-element.51.keep_ref, bf16[3072,128]{1,0:T(8,128)(2,1)S(1)} %collective-permute-done.6.come_ref), custom_call_target="tpu_custom_call" | custom-call | tf_op jit(solution)/shard_map/pallas_call | solution.py:194
  62.7 0.0 all-to-all-done.1
  62.7 5.8 %all-to-all-start.2 = ((bf16[32,32,640]{2,1,0:T(8,128)(2,1)}), bf16[32,32,640]{2,1,0:T(8,128)(2,1)S(1)}, u32[]{:S(2)}, u32[]{:S(2)}) async-start(bf16[32,32,640]{2,1,0:T(8,128)(2,1)} %bitcast.29), calls=%async_computation.2 | async-start | bytes 2621440 | tf_op jit(solution)/shard_map/all_to_all | solution.py:576
  68.5 0.1 add_add_fusion.info
  68.5 2.8 %shard_map.183 = (f32[8,128,256]{2,1,0:T(8,128)S(1)}, f32[8,128,256]{2,1,0:T(8,128)S(1)}, f32[16,256]{1,0:T(8,128)S(1)}, bf16[144,256]{1,0:T(8,128)(2,1)S(1)}, b...) custom-call(s32[4,8]{1,0:T(4,128)S(1)} %add_add_fusion.info, ...), custom_call_target="tpu_custom_call" | custom-call | flops 3000000000 | bytes 1000000 | tf_op jit(solution)/shard_map/pallas_call | solution.py:287
  71.4 7.1 %collective-permute-start.8 = (bf16[144,256]{1,0:T(8,128)(2,1)S(1)}, bf16[144,256]{1,0:T(8,128)(2,1)S(1)}, u32[]{:S(2)}, u32[]{:S(2)}) collective-permute-start(bf16[144,256]{1,0:T(8,128)(2,1)S(1)} %get-tuple-element.64), channel_id=1, source_target_pairs={{0,64},{32,96},{64,128},{96,160},{128,192},{160,224},{1,65},{33,97... | collective-permute-start | bytes 221192 | tf_op jit(solution)/shard_map/ppermute | solution.py:572
  78.5 5.3 %collective-permute-start.7 = (bf16[144,256]{1,0:T(8,128)(2,1)S(1)}, bf16[144,256]{1,0:T(8,128)(2,1)S(1)}, u32[]{:S(2)}, u32[]{:S(2)}) collective-permute-start(bf16[144,256]{1,0:T(8,128)(2,1)S(1)} %get-tuple-element.64), channel_id=1, source_target_pairs={{0,32},{32,64},{64,96},{96,128},{128,160},{160,192},{192,224},{1,3... | collective-permute-start | bytes 221192 | tf_op jit(solution)/shard_map/ppermute | solution.py:572
  83.8 1.9 %collective-permute-start.10 = (bf16[144,256]{1,0:T(8,128)(2,1)S(1)}, bf16[144,256]{1,0:T(8,128)(2,1)S(1)}, u32[]{:S(2)}, u32[]{:S(2)}) collective-permute-start(bf16[144,256]{1,0:T(8,128)(2,1)S(1)} %get-tuple-element.65), channel_id=1, source_target_pairs={{64,0},{96,32},{128,64},{160,96},{192,128},{224,160},{65,1},{97,33... | collective-permute-start | bytes 221192 | tf_op jit(solution)/shard_map/ppermute | solution.py:572
  85.7 1.9 %collective-permute-start.9 = (bf16[144,256]{1,0:T(8,128)(2,1)S(1)}, bf16[144,256]{1,0:T(8,128)(2,1)S(1)}, u32[]{:S(2)}, u32[]{:S(2)}) collective-permute-start(bf16[144,256]{1,0:T(8,128)(2,1)S(1)} %get-tuple-element.65), channel_id=1, source_target_pairs={{32,0},{64,32},{96,64},{128,96},{160,128},{192,160},{224,192},{33,... | collective-permute-start | bytes 221192 | tf_op jit(solution)/shard_map/ppermute | solution.py:572
  87.6 7.6 %shard_map.184.part_ref = f32[1024,768]{1,0:T(8,128)S(1)} custom-call(s32[4,8]{1,0:T(4,128)S(1)} %add_add_fusion.info, f32[4]{0:T(128)S(1)} %get-tuple-element.55.rates, f32[4]{0:T(128)S(1)} %get-tuple-element.58.skips, bf16[1024,896]{1,0:T(8,128)(2,1)S(1)} %bitcast.24, s32[8,128]{1,0:T(8,128)S(1)} %bitcast_subtract_fusion.ends_ref), custom_call_target="tpu_custom_call" | custom-call | flops 8000000000 | bytes 1000000 | tf_op jit(solution)/shard_map/pallas_call | solution.py:369
  95.3 0.0 collective-permute-done.8.f2
  95.3 0.0 collective-permute-done.7.f1
  95.3 0.0 collective-permute-done.10.b2
  95.3 0.0 collective-permute-done.9.b1
  95.3 1.9 %shard_map.185 = bf16[1024,768]{1,0:T(8,128)(2,1)} custom-call(bf16[1024,896]{1,0:T(8,128)(2,1)S(1)} %bitcast.25, f32[1024,768]{1,0:T(8,128)S(1)} %shard_map.184.part_ref, bf16[1024,512]{1,0:T(8,128)(2,1)S(1)} %get-tuple-element.59.low_ref, f32[1024,512]{1,0:T(8,128)S(1)} %get-tuple-element.60.full_ref, f32[8,128,256]{2,1,0:T(8,128)S(1)} %get-tuple-element.61.inc_ref, ...), custom_call_target="tpu_custom_call" | custom-call | flops 2000000000 | bytes 1000000 | tf_op jit(solution)/shard_map/pallas_call | solution.py:401
  97.3 0.0 all-to-all-done.2.in_ref
  97.3 7.4 %all-to-all-start.3 = ((bf16[32,32,768]{2,1,0:T(8,128)(2,1)}), bf16[32,32,768]{2,1,0:T(8,128)(2,1)S(1)}, u32[]{:S(2)}, u32[]{:S(2)}) async-start(bf16[32,32,768]{2,1,0:T(8,128)(2,1)} %bitcast.28), calls=%async_computation.3 | async-start | bytes 3145728 | tf_op jit(solution)/shard_map/all_to_all | solution.py:576
  104.6 1.5 %shard_map.187 = (bf16[32,4096]{1,0:T(8,128)(2,1)}, bf16[32,4096]{1,0:T(8,128)(2,1)}, bf16[32,2048]{1,0:T(8,128)(2,1)S(1)}, bf16[32,2048]{1,0:T(8,128)(2,1)S(1)}, f32[32,2048]{1,0:T(8,128)S(1)}) custom-call(bf16[32,32,640]{2,1,0:T(8,128)(2,1)S(1)} %all-to-all-done.2.in_ref), custom_call_target="tpu_custom_call" | custom-call | tf_op jit(solution)/shard_map/pallas_call | solution.py:151
  106.1 1.9 %collective-permute-start.11 = (bf16[32,2048]{1,0:T(8,128)(2,1)S(1)}, bf16[32,2048]{1,0:T(8,128)(2,1)S(1)}, u32[]{:S(2)}, u32[]{:S(2)}) collective-permute-start(bf16[32,2048]{1,0:T(8,128)(2,1)S(1)} %get-tuple-element.76), channel_id=1, source_target_pairs={{32,0},{64,32},{96,64},{128,96},{160,128},{192,160},{224,192},{33,... | collective-permute-start | bytes 393224 | tf_op jit(solution)/shard_map/ppermute | solution.py:572
  108.0 1.9 %collective-permute-start.12 = (bf16[32,2048]{1,0:T(8,128)(2,1)S(1)}, bf16[32,2048]{1,0:T(8,128)(2,1)S(1)}, u32[]{:S(2)}, u32[]{:S(2)}) collective-permute-start(bf16[32,2048]{1,0:T(8,128)(2,1)S(1)} %get-tuple-element.77), channel_id=1, source_target_pairs={{64,0},{96,32},{128,64},{160,96},{192,128},{224,160},{65,1},{97,33... | collective-permute-start | bytes 393224 | tf_op jit(solution)/shard_map/ppermute | solution.py:572
  109.9 4.3 %collective-permute-done.11.one_ref = bf16[32,2048]{1,0:T(8,128)(2,1)S(1)} collective-permute-done((bf16[32,2048]{1,0:T(8,128)(2,1)S(1)}, bf16[32,2048]{1,0:T(8,128)(2,1)S(1)}, u32[]{:S(2)}, u32[]{:S(2)}) %collective-permute-start.11) | collective-permute-done | bytes 131104 | tf_op jit(solution)/shard_map/ppermute | solution.py:572
  114.3 7.7 %collective-permute-done.12.two_ref = bf16[32,2048]{1,0:T(8,128)(2,1)S(1)} collective-permute-done((bf16[32,2048]{1,0:T(8,128)(2,1)S(1)}, bf16[32,2048]{1,0:T(8,128)(2,1)S(1)}, u32[]{:S(2)}, u32[]{:S(2)}) %collective-permute-start.12) | collective-permute-done | bytes 131104 | tf_op jit(solution)/shard_map/ppermute | solution.py:572
  121.9 0.7 shard_map.188
  122.6 4.5 %all-to-all-done.3.in_ref = bf16[32,32,768]{2,1,0:T(8,128)(2,1)S(1)} async-done(((bf16[32,32,768]{2,1,0:T(8,128)(2,1)}), bf16[32,32,768]{2,1,0:T(8,128)(2,1)S(1)}, u32[]{:S(2)}, u32[]{:S(2)}) %all-to-all-start.3) | async-done | bytes 1572896 | tf_op jit(solution)/shard_map/all_to_all | solution.py:576
  127.1 1.6 %shard_map.186 = (bf16[32,8192]{1,0:T(8,128)(2,1)}, bf16[32,8192]{1,0:T(8,128)(2,1)}, bf16[32,1024]{1,0:T(8,128)(2,1)}, bf16[32,1024]{1,0:T(8,128)(2,1)}) custom-call(bf16[32,32,768]{2,1,0:T(8,128)(2,1)S(1)} %all-to-all-done.3.in_ref), custom_call_target="tpu_custom_call" | custom-call | tf_op jit(solution)/shard_map/pallas_call | solution.py:120
  (11 shorter events, 0.1 us)
Async XLA Ops:
  0.6 10.6 %copy-start.2 = (f32[32]{0:T(128)S(1)}, f32[32]{0:T(128)}, u32[]{:S(2)}) copy-start(f32[32]{0:T(128)} %param.16) | copy-start | bytes 388
  0.6 10.6 %copy-start.1 = (f32[32]{0:T(128)S(1)}, f32[32]{0:T(128)}, u32[]{:S(2)}) copy-start(f32[32]{0:T(128)} %param.17) | copy-start | bytes 388
  0.7 11.3 %copy-start = (s32[64]{0:T(128)S(1)}, s32[64]{0:T(128)}, u32[]{:S(2)}) copy-start(s32[64]{0:T(128)} %param.21) | copy-start | bytes 772
  3.9 21.7 %all-to-all-start = ((bf16[32,32,384]{2,1,0:T(8,128)(2,1)}), bf16[32,32,384]{2,1,0:T(8,128)(2,1)S(1)}, u32[]{:S(2)}, u32[]{:S(2)}) async-start(bf16[32,32,384]{2,1,0:T(8,128)(2,1)} %shard_map.179), calls=%async_computation | async-start | bytes 1572864 | tf_op jit(solution)/shard_map/all_to_all | solution.py:576
  11.3 18.3 %collective-permute-start.3 = (f32[2,32]{1,0:T(2,128)S(1)}, f32[2,32]{1,0:T(2,128)S(1)}, u32[]{:S(2)}, u32[]{:S(2)}) collective-permute-start(f32[2,32]{1,0:T(2,128)S(1)} %pad_maximum_fusion), channel_id=1, source_target_pairs={{0,0},{1,8},{2,16},{3,24},{8,1},{9,9},{10,17},{11,25},{16,2},{17,1... | collective-permute-start | bytes 776 | tf_op jit(solution)/shard_map/ppermute | solution.py:592
  25.7 4.0 %collective-permute-start.2 = (bf16[1024,128]{1,0:T(8,128)(2,1)S(1)}, bf16[1024,128]{1,0:T(8,128)(2,1)S(1)}, u32[]{:S(2)}, u32[]{:S(2)}) collective-permute-start(bf16[1024,128]{1,0:T(8,128)(2,1)S(1)} %slice.16.own0), channel_id=1, source_target_pairs={{0,4},{4,0},{1,5},{5,1},{2,6},{6,2},{3,7},{7,3},{8,12},{12,8},{9,1... | collective-permute-start | bytes 786440 | tf_op jit(solution)/shard_map/ppermute | solution.py:580
  25.8 10.7 %collective-permute-start = (bf16[1024,128]{1,0:T(8,128)(2,1)S(1)}, bf16[1024,128]{1,0:T(8,128)(2,1)}, u32[]{:S(2)}, u32[]{:S(2)}) collective-permute-start(bf16[1024,128]{1,0:T(8,128)(2,1)S(1)} %slice.16.own0), channel_id=1, source_target_pairs={{0,32},{32,64},{64,96},{96,128},{128,160},{160,192},{192,224},{1,3... | collective-permute-start | bytes 786440 | tf_op jit(solution)/shard_map/ppermute | solution.py:572
  29.7 33.0 %all-to-all-start.1 = ((bf16[32,32,896]{2,1,0:T(8,128)(2,1)}), bf16[32,32,896]{2,1,0:T(8,128)(2,1)S(1)}, u32[]{:S(2)}, u32[]{:S(2)}) async-start(bf16[32,32,896]{2,1,0:T(8,128)(2,1)} %shard_map.180), calls=%async_computation.1 | async-start | bytes 3670016 | tf_op jit(solution)/shard_map/all_to_all | solution.py:576
  36.5 10.1 %collective-permute-start.1 = (bf16[1024,128]{1,0:T(8,128)(2,1)}, bf16[1024,128]{1,0:T(8,128)(2,1)}, u32[]{:S(2)}, u32[]{:S(2)}) collective-permute-start(bf16[1024,128]{1,0:T(8,128)(2,1)} %collective-permute-done.own1), channel_id=1, source_target_pairs={{0,32},{32,64},{64,96},{96,128},{128,160},{160,192},{192,224},{1,3... | collective-permute-start | bytes 786440 | tf_op jit(solution)/shard_map/ppermute | solution.py:572
  41.0 5.7 %collective-permute-start.4 = (bf16[1024,128]{1,0:T(8,128)(2,1)}, bf16[1024,128]{1,0:T(8,128)(2,1)}, u32[]{:S(2)}, u32[]{:S(2)}) collective-permute-start(bf16[1024,128]{1,0:T(8,128)(2,1)} %collective-permute-done.own1), channel_id=1, source_target_pairs={{0,4},{4,0},{1,5},{5,1},{2,6},{6,2},{3,7},{7,3},{8,12},{12,8},{9,1... | collective-permute-start | bytes 786440 | tf_op jit(solution)/shard_map/ppermute | solution.py:580
  46.6 1.9 %collective-permute-start.5 = (bf16[1024,128]{1,0:T(8,128)(2,1)}, bf16[1024,128]{1,0:T(8,128)(2,1)}, u32[]{:S(2)}, u32[]{:S(2)}) collective-permute-start(bf16[1024,128]{1,0:T(8,128)(2,1)} %collective-permute-done.1.own2), channel_id=1, source_target_pairs={{0,4},{4,0},{1,5},{5,1},{2,6},{6,2},{3,7},{7,3},{8,12},{12,8},{9,1... | collective-permute-start | bytes 786440 | tf_op jit(solution)/shard_map/ppermute | solution.py:580
  57.3 2.8 %collective-permute-start.6 = (bf16[3072,128]{1,0:T(8,128)(2,1)}, bf16[3072,128]{1,0:T(8,128)(2,1)S(1)}, u32[]{:S(2)}, u32[]{:S(2)}) collective-permute-start(bf16[3072,128]{1,0:T(8,128)(2,1)} %get-tuple-element.52), channel_id=1, source_target_pairs={{0,4},{4,0},{1,5},{5,1},{2,6},{6,2},{3,7},{7,3},{8,12},{12,8},{9,1... | collective-permute-start | bytes 2359304 | tf_op jit(solution)/shard_map/ppermute | solution.py:580
  62.7 34.6 %all-to-all-start.2 = ((bf16[32,32,640]{2,1,0:T(8,128)(2,1)}), bf16[32,32,640]{2,1,0:T(8,128)(2,1)S(1)}, u32[]{:S(2)}, u32[]{:S(2)}) async-start(bf16[32,32,640]{2,1,0:T(8,128)(2,1)} %bitcast.29), calls=%async_computation.2 | async-start | bytes 2621440 | tf_op jit(solution)/shard_map/all_to_all | solution.py:576
  71.4 23.9 %collective-permute-start.8 = (bf16[144,256]{1,0:T(8,128)(2,1)S(1)}, bf16[144,256]{1,0:T(8,128)(2,1)S(1)}, u32[]{:S(2)}, u32[]{:S(2)}) collective-permute-start(bf16[144,256]{1,0:T(8,128)(2,1)S(1)} %get-tuple-element.64), channel_id=1, source_target_pairs={{0,64},{32,96},{64,128},{96,160},{128,192},{160,224},{1,65},{33,97... | collective-permute-start | bytes 221192 | tf_op jit(solution)/shard_map/ppermute | solution.py:572
  78.5 16.8 %collective-permute-start.7 = (bf16[144,256]{1,0:T(8,128)(2,1)S(1)}, bf16[144,256]{1,0:T(8,128)(2,1)S(1)}, u32[]{:S(2)}, u32[]{:S(2)}) collective-permute-start(bf16[144,256]{1,0:T(8,128)(2,1)S(1)} %get-tuple-element.64), channel_id=1, source_target_pairs={{0,32},{32,64},{64,96},{96,128},{128,160},{160,192},{192,224},{1,3... | collective-permute-start | bytes 221192 | tf_op jit(solution)/shard_map/ppermute | solution.py:572
  83.8 11.5 %collective-permute-start.10 = (bf16[144,256]{1,0:T(8,128)(2,1)S(1)}, bf16[144,256]{1,0:T(8,128)(2,1)S(1)}, u32[]{:S(2)}, u32[]{:S(2)}) collective-permute-start(bf16[144,256]{1,0:T(8,128)(2,1)S(1)} %get-tuple-element.65), channel_id=1, source_target_pairs={{64,0},{96,32},{128,64},{160,96},{192,128},{224,160},{65,1},{97,33... | collective-permute-start | bytes 221192 | tf_op jit(solution)/shard_map/ppermute | solution.py:572
  85.7 9.6 %collective-permute-start.9 = (bf16[144,256]{1,0:T(8,128)(2,1)S(1)}, bf16[144,256]{1,0:T(8,128)(2,1)S(1)}, u32[]{:S(2)}, u32[]{:S(2)}) collective-permute-start(bf16[144,256]{1,0:T(8,128)(2,1)S(1)} %get-tuple-element.65), channel_id=1, source_target_pairs={{32,0},{64,32},{96,64},{128,96},{160,128},{192,160},{224,192},{33,... | collective-permute-start | bytes 221192 | tf_op jit(solution)/shard_map/ppermute | solution.py:572
  97.3 29.9 %all-to-all-start.3 = ((bf16[32,32,768]{2,1,0:T(8,128)(2,1)}), bf16[32,32,768]{2,1,0:T(8,128)(2,1)S(1)}, u32[]{:S(2)}, u32[]{:S(2)}) async-start(bf16[32,32,768]{2,1,0:T(8,128)(2,1)} %bitcast.28), calls=%async_computation.3 | async-start | bytes 3145728 | tf_op jit(solution)/shard_map/all_to_all | solution.py:576
  106.1 8.2 %collective-permute-start.11 = (bf16[32,2048]{1,0:T(8,128)(2,1)S(1)}, bf16[32,2048]{1,0:T(8,128)(2,1)S(1)}, u32[]{:S(2)}, u32[]{:S(2)}) collective-permute-start(bf16[32,2048]{1,0:T(8,128)(2,1)S(1)} %get-tuple-element.76), channel_id=1, source_target_pairs={{32,0},{64,32},{96,64},{128,96},{160,128},{192,160},{224,192},{33,... | collective-permute-start | bytes 393224 | tf_op jit(solution)/shard_map/ppermute | solution.py:572
  108.0 13.9 %collective-permute-start.12 = (bf16[32,2048]{1,0:T(8,128)(2,1)S(1)}, bf16[32,2048]{1,0:T(8,128)(2,1)S(1)}, u32[]{:S(2)}, u32[]{:S(2)}) collective-permute-start(bf16[32,2048]{1,0:T(8,128)(2,1)S(1)} %get-tuple-element.77), channel_id=1, source_target_pairs={{64,0},{96,32},{128,64},{160,96},{192,128},{224,160},{65,1},{97,33... | collective-permute-start | bytes 393224 | tf_op jit(solution)/shard_map/ppermute | solution.py:572
